TPU v7x, 512 devices: a whole 4x4x16 slice. The times are simulated.
512 devices in a mesh: seq: 128 (over z_lo, x, y), grp: 4 (over z_hi, core).
Axes of the slice: x: 4, y: 4, z: 16 (z_hi: 2, z_lo: 8; z = z_hi * 8 + z_lo), core: 2. Of those that a mesh axis runs over, the one named last changes fastest.
Arguments:
- queries: bfloat16 [81920, 2048], P(('grp', 'seq')), parts along dimension 0, may hold values from -6 to 6
- keys: bfloat16 [81920, 2048], P(('grp', 'seq')), parts along dimension 0, may hold values from -6 to 6
- values: bfloat16 [81920, 2048], P(('grp', 'seq')), parts along dimension 0, may hold values from -6 to 6
- out_grad: bfloat16 [81920, 2048], P(('grp', 'seq')), parts along dimension 0, may hold values from -6 to 6
- log_sum: float32 [16, 81920], P(None, ('grp', 'seq')), parts along dimension 1, may hold values from 3.5 to 4.5
- delta: float32 [16, 81920], P(None, ('grp', 'seq')), parts along dimension 1, may hold values from -24 to 24
Outputs:
- query_grad: bfloat16 [81920, 2048], P(('grp', 'seq')), parts along dimension 0
- key_grad: bfloat16 [81920, 2048], P(('grp', 'seq')), parts along dimension 0
- value_grad: bfloat16 [81920, 2048], P(('grp', 'seq')), parts along dimension 0
There are 4 independent parts, one for each index of `grp`. A program takes and returns all parts, laid end to end along the dimension named above; each array names one. Nothing has to cross between parts.
All inputs are finite; a program needn't handle non-finite values.
Results may differ from a plain program's by a relative error of at most 0.04.
Values may be sent and summed in bfloat16 or wider, within the bound.
No kernel may reach another device: no remote copies, remote signals or barrier semaphores. Data moves between devices by JAX's collectives and lax.ppermute only.
A program may use at most 64 MiB of HBM per device.

v0:
```python
import jax
import jax.numpy as jnp
from jax import lax
from jax.sharding import PartitionSpec as P


def from_behind(shard, axis, by):
    devices = lax.axis_size(axis)
    pairs = [(i, i + by) for i in range(devices) if 0 <= i + by < devices]
    return lax.ppermute(shard, axis, pairs)


def block_terms(q_rows, grad_rows, lse_rows, delta_rows, k_rows, v_rows, keep_mask):
    heads = lse_rows.shape[0]
    row_count, width = q_rows.shape
    depth = width // heads
    scale = depth ** (-0.5)
    q_heads = q_rows.reshape(row_count, heads, depth)
    g_heads = grad_rows.reshape(row_count, heads, depth)
    k_heads = k_rows.reshape(row_count, heads, depth)
    v_heads = v_rows.reshape(row_count, heads, depth)
    scores = (
        jnp.einsum("shd,thd->hst", q_heads, k_heads, preferred_element_type=jnp.float32) * scale
    )
    prob = jnp.where(keep_mask[None], jnp.exp(scores - lse_rows[:, :, None]), jnp.float32(0.0))
    dprob = jnp.einsum("shd,thd->hst", g_heads, v_heads, preferred_element_type=jnp.float32)
    dscore = prob * (dprob - delta_rows[:, :, None])
    prob_b = prob.astype(jnp.bfloat16)
    dscore_b = dscore.astype(jnp.bfloat16)
    query_term = (
        jnp.einsum("hst,thd->shd", dscore_b, k_heads, preferred_element_type=jnp.float32) * scale
    )
    key_term = (
        jnp.einsum("hst,shd->thd", dscore_b, q_heads, preferred_element_type=jnp.float32) * scale
    )
    value_term = jnp.einsum("hst,shd->thd", prob_b, g_heads, preferred_element_type=jnp.float32)
    return (
        query_term.reshape(row_count, width),
        key_term.reshape(row_count, width),
        value_term.reshape(row_count, width),
    )


def on_device(queries, keys, values, out_grad, log_sum, delta):
    device_count = lax.axis_size("seq")
    position = lax.axis_index("seq")
    row_count = queries.shape[0]
    row_ids = lax.broadcasted_iota(jnp.int32, (row_count, row_count), 0)
    col_ids = lax.broadcasted_iota(jnp.int32, (row_count, row_count), 1)
    causal = row_ids >= col_ids
    everything = jnp.ones((row_count, row_count), dtype=bool)
    query_acc, key_acc, value_acc = block_terms(
        queries, out_grad, log_sum, delta, keys, values, causal
    )
    first_step = device_count // 4
    for offset in (first_step, first_step + 1):
        for distance in (offset, device_count - offset):
            far_keys, far_values = from_behind((keys, values), "seq", distance)
            keep_mask = jnp.logical_and(everything, position >= distance)
            part_q, part_k, part_v = block_terms(
                queries, out_grad, log_sum, delta, far_keys, far_values, keep_mask
            )
            query_acc = query_acc + lax.optimization_barrier(part_q.astype(jnp.bfloat16)).astype(
                jnp.float32
            )
            back_keys, back_values = from_behind(
                (part_k.astype(jnp.bfloat16), part_v.astype(jnp.bfloat16)), "seq", -distance
            )
            key_acc = key_acc + back_keys.astype(jnp.float32)
            value_acc = value_acc + back_values.astype(jnp.float32)
    return (
        query_acc.astype(jnp.bfloat16),
        key_acc.astype(jnp.bfloat16),
        value_acc.astype(jnp.bfloat16),
    )


def solution(mesh):
    in_specs = (
        P(("grp", "seq"), None),
        P(("grp", "seq"), None),
        P(("grp", "seq"), None),
        P(("grp", "seq"), None),
        P(None, ("grp", "seq")),
        P(None, ("grp", "seq")),
    )
    out_specs = (P(("grp", "seq"), None), P(("grp", "seq"), None), P(("grp", "seq"), None))
    return jax.shard_map(
        on_device, mesh=mesh, in_specs=in_specs, out_specs=out_specs, check_vma=False
    )
```

profile of v0, /device:TPU:22, one launch (start us, length us, event | category | flops | bytes accessed | tf_op | source)
XLA Modules:
  0.0 555.4 jit_solution(1839106369802498050)
XLA Ops:
  0.6 12.8 %collective-permute-start.3 = (bf16[160,2048]{1,0:T(8,128)(2,1)}, bf16[160,2048]{1,0:T(8,128)(2,1)}, u32[]{:S(2)}, u32[]{:S(2)}) collective-permute-start(bf16[160,2048]{1,0:T(8,128)(2,1)} %param.8), channel_id=1, source_target_pairs={{0,384},{4,388},{8,392},{12,396},{16,400},{20,404},{24,408},{28,41... | collective-permute-start | bytes 1966088 | tf_op jit(solution)/shard_map/ppermute | solution.py:10
  13.4 2.1 collective-permute-start.1
  15.5 2.1 collective-permute-start.7
  17.7 2.1 collective-permute-start.5
  19.8 3.0 collective-permute-start.4
  22.9 1.9 fusion.105
  26.0 1.6 fusion.6
  27.6 2.5 convolution_bitcast_fusion
  30.9 52.3 %collective-permute-done.4 = bf16[160,2048]{1,0:T(8,128)(2,1)} collective-permute-done((bf16[160,2048]{1,0:T(8,128)(2,1)}, bf16[160,2048]{1,0:T(8,128)(2,1)}, u32[]{:S(2)}, u32[]{:S(2)}) %collective-permute-start.4) | collective-permute-done | bytes 655392 | tf_op jit(solution)/shard_map/ppermute | solution.py:10
  83.2 6.5 %collective-permute-start.6 = (bf16[160,2048]{1,0:T(8,128)(2,1)S(1)}, bf16[160,2048]{1,0:T(8,128)(2,1)S(1)}, u32[]{:S(2)}, u32[]{:S(2)}) collective-permute-start(bf16[160,2048]{1,0:T(8,128)(2,1)S(1)} %copy-done.3), channel_id=1, source_target_pairs={{0,380},{4,384},{8,388},{12,392},{16,396},{20,400},{24,404},{28,40... | collective-permute-start | bytes 1966088 | tf_op jit(solution)/shard_map/ppermute | solution.py:10
  89.6 1.6 fusion.80
  91.3 1.5 fusion.66
  92.7 1.4 collective-permute-start.2
  94.1 2.5 multiply_convert_fusion.1
  96.6 8.2 %collective-permute-done.6 = bf16[160,2048]{1,0:T(8,128)(2,1)S(1)} collective-permute-done((bf16[160,2048]{1,0:T(8,128)(2,1)S(1)}, bf16[160,2048]{1,0:T(8,128)(2,1)S(1)}, u32[]{:S(2)}, u32[]{:S(2)}) %collective-permute-start.6) | collective-permute-done | bytes 655392 | tf_op jit(solution)/shard_map/ppermute | solution.py:10
  106.7 1.6 fusion.57
  108.3 1.5 fusion.69
  111.0 19.9 %collective-permute-done = bf16[160,2048]{1,0:T(8,128)(2,1)S(1)} collective-permute-done((bf16[160,2048]{1,0:T(8,128)(2,1)S(1)}, bf16[160,2048]{1,0:T(8,128)(2,1)S(1)}, u32[]{:S(2)}, u32[]{:S(2)}) %collective-permute-start) | collective-permute-done | bytes 655392 | tf_op jit(solution)/shard_map/ppermute | solution.py:10
  132.8 1.5 fusion.60
  134.3 1.5 collective-permute-start.14
  135.8 2.5 multiply_convert_fusion
  140.6 1.5 fusion.63
  144.5 2.5 multiply_convert_fusion.3
  148.8 2.5 multiply_convert_fusion.2
  154.5 168.5 %collective-permute-done.14 = bf16[160,2048]{1,0:T(8,128)(2,1)S(1)} collective-permute-done((bf16[160,2048]{1,0:T(8,128)(2,1)S(1)}, bf16[160,2048]{1,0:T(8,128)(2,1)S(1)}, u32[]{:S(2)}, u32[]{:S(2)}) %collective-permute-start.14) | collective-permute-done | bytes 655392 | tf_op jit(solution)/shard_map/ppermute | solution.py:10
  325.6 1.4 collective-permute-start.9
  327.0 1.3 fusion.31
  328.3 64.1 %collective-permute-done.13 = bf16[160,2048]{1,0:T(8,128)(2,1)S(1)} collective-permute-done((bf16[160,2048]{1,0:T(8,128)(2,1)S(1)}, bf16[160,2048]{1,0:T(8,128)(2,1)S(1)}, u32[]{:S(2)}, u32[]{:S(2)}) %collective-permute-start.13) | collective-permute-done | bytes 655392 | tf_op jit(solution)/shard_map/ppermute | solution.py:10
  392.4 1.3 fusion.23
  393.8 20.8 %collective-permute-done.8 = bf16[160,2048]{1,0:T(8,128)(2,1)S(1)} collective-permute-done((bf16[160,2048]{1,0:T(8,128)(2,1)S(1)}, bf16[160,2048]{1,0:T(8,128)(2,1)S(1)}, u32[]{:S(2)}, u32[]{:S(2)}) %collective-permute-start.8) | collective-permute-done | bytes 655392 | tf_op jit(solution)/shard_map/ppermute | solution.py:10
  414.6 139.5 %collective-permute-done.9 = bf16[160,2048]{1,0:T(8,128)(2,1)S(1)} collective-permute-done((bf16[160,2048]{1,0:T(8,128)(2,1)S(1)}, bf16[160,2048]{1,0:T(8,128)(2,1)S(1)}, u32[]{:S(2)}, u32[]{:S(2)}) %collective-permute-start.9) | collective-permute-done | bytes 655392 | tf_op jit(solution)/shard_map/ppermute | solution.py:10
  554.1 1.3 fusion.27
  (57 shorter events, 19.0 us)
Async XLA Ops:
  0.6 24.1 %copy-start = (bf16[160,2048]{1,0:T(8,128)(2,1)S(1)}, bf16[160,2048]{1,0:T(8,128)(2,1)}, u32[]{:S(2)}) copy-start(bf16[160,2048]{1,0:T(8,128)(2,1)} %param.9) | copy-start | bytes 1966084
  0.6 146.8 %collective-permute-start.3 = (bf16[160,2048]{1,0:T(8,128)(2,1)}, bf16[160,2048]{1,0:T(8,128)(2,1)}, u32[]{:S(2)}, u32[]{:S(2)}) collective-permute-start(bf16[160,2048]{1,0:T(8,128)(2,1)} %param.8), channel_id=1, source_target_pairs={{0,384},{4,388},{8,392},{12,396},{16,400},{20,404},{24,408},{28,41... | collective-permute-start | bytes 1966088 | tf_op jit(solution)/shard_map/ppermute | solution.py:10
  13.4 129.7 %collective-permute-start.1 = (bf16[160,2048]{1,0:T(8,128)(2,1)}, bf16[160,2048]{1,0:T(8,128)(2,1)}, u32[]{:S(2)}, u32[]{:S(2)}) collective-permute-start(bf16[160,2048]{1,0:T(8,128)(2,1)} %param.8), channel_id=1, source_target_pairs={{0,128},{4,132},{8,136},{12,140},{16,144},{20,148},{24,152},{28,15... | collective-permute-start | bytes 1966088 | tf_op jit(solution)/shard_map/ppermute | solution.py:10
  15.5 118.7 %collective-permute-start.7 = (bf16[160,2048]{1,0:T(8,128)(2,1)}, bf16[160,2048]{1,0:T(8,128)(2,1)}, u32[]{:S(2)}, u32[]{:S(2)}) collective-permute-start(bf16[160,2048]{1,0:T(8,128)(2,1)} %param.8), channel_id=1, source_target_pairs={{0,380},{4,384},{8,388},{12,392},{16,396},{20,400},{24,404},{28,40... | collective-permute-start | bytes 1966088 | tf_op jit(solution)/shard_map/ppermute | solution.py:10
  17.7 75.1 %collective-permute-start.5 = (bf16[160,2048]{1,0:T(8,128)(2,1)}, bf16[160,2048]{1,0:T(8,128)(2,1)}, u32[]{:S(2)}, u32[]{:S(2)}) collective-permute-start(bf16[160,2048]{1,0:T(8,128)(2,1)} %param.8), channel_id=1, source_target_pairs={{0,132},{4,136},{8,140},{12,144},{16,148},{20,152},{24,156},{28,16... | collective-permute-start | bytes 1966088 | tf_op jit(solution)/shard_map/ppermute | solution.py:10
  19.8 63.4 %collective-permute-start.4 = (bf16[160,2048]{1,0:T(8,128)(2,1)}, bf16[160,2048]{1,0:T(8,128)(2,1)}, u32[]{:S(2)}, u32[]{:S(2)}) collective-permute-start(bf16[160,2048]{1,0:T(8,128)(2,1)} %param.7), channel_id=1, source_target_pairs={{0,132},{4,136},{8,140},{12,144},{16,148},{20,152},{24,156},{28,16... | collective-permute-start | bytes 1966088 | tf_op jit(solution)/shard_map/ppermute | solution.py:10
  22.9 1.9 copy-start.5
  22.9 1.9 copy-start.6
  22.9 1.9 copy-start.7
  24.8 1.2 copy-start.3
  27.6 2.6 copy-start.1
  83.2 21.7 %collective-permute-start.6 = (bf16[160,2048]{1,0:T(8,128)(2,1)S(1)}, bf16[160,2048]{1,0:T(8,128)(2,1)S(1)}, u32[]{:S(2)}, u32[]{:S(2)}) collective-permute-start(bf16[160,2048]{1,0:T(8,128)(2,1)S(1)} %copy-done.3), channel_id=1, source_target_pairs={{0,380},{4,384},{8,388},{12,392},{16,396},{20,400},{24,404},{28,40... | collective-permute-start | bytes 1966088 | tf_op jit(solution)/shard_map/ppermute | solution.py:10
  92.7 45.5 %collective-permute-start.2 = (bf16[160,2048]{1,0:T(8,128)(2,1)S(1)}, bf16[160,2048]{1,0:T(8,128)(2,1)S(1)}, u32[]{:S(2)}, u32[]{:S(2)}) collective-permute-start(bf16[160,2048]{1,0:T(8,128)(2,1)S(1)} %copy-done.3), channel_id=1, source_target_pairs={{0,384},{4,388},{8,392},{12,396},{16,400},{20,404},{24,408},{28,41... | collective-permute-start | bytes 1966088 | tf_op jit(solution)/shard_map/ppermute | solution.py:10
  104.9 26.1 %collective-permute-start = (bf16[160,2048]{1,0:T(8,128)(2,1)S(1)}, bf16[160,2048]{1,0:T(8,128)(2,1)S(1)}, u32[]{:S(2)}, u32[]{:S(2)}) collective-permute-start(bf16[160,2048]{1,0:T(8,128)(2,1)S(1)} %copy-done.3), channel_id=1, source_target_pairs={{0,128},{4,132},{8,136},{12,140},{16,144},{20,148},{24,152},{28,15... | collective-permute-start | bytes 1966088 | tf_op jit(solution)/shard_map/ppermute | solution.py:10
  131.0 262.8 %collective-permute-start.10 = (bf16[160,2048]{1,0:T(8,128)(2,1)S(1)}, bf16[160,2048]{1,0:T(8,128)(2,1)S(1)}, u32[]{:S(2)}, u32[]{:S(2)}) collective-permute-start(bf16[160,2048]{1,0:T(8,128)(2,1)S(1)} %bitcast.324), channel_id=1, source_target_pairs={{132,0},{136,4},{140,8},{144,12},{148,16},{152,20},{156,24},{160,2... | collective-permute-start | bytes 1966088 | tf_op jit(solution)/shard_map/ppermute | solution.py:10
  134.3 188.7 %collective-permute-start.14 = (bf16[160,2048]{1,0:T(8,128)(2,1)S(1)}, bf16[160,2048]{1,0:T(8,128)(2,1)S(1)}, u32[]{:S(2)}, u32[]{:S(2)}) collective-permute-start(bf16[160,2048]{1,0:T(8,128)(2,1)S(1)} %bitcast.326), channel_id=1, source_target_pairs={{132,0},{136,4},{140,8},{144,12},{148,16},{152,20},{156,24},{160,2... | collective-permute-start | bytes 1966088 | tf_op jit(solution)/shard_map/ppermute | solution.py:10
  138.3 186.0 %collective-permute-start.15 = (bf16[160,2048]{1,0:T(8,128)(2,1)S(1)}, bf16[160,2048]{1,0:T(8,128)(2,1)S(1)}, u32[]{:S(2)}, u32[]{:S(2)}) collective-permute-start(bf16[160,2048]{1,0:T(8,128)(2,1)S(1)} %bitcast.325), channel_id=1, source_target_pairs={{380,0},{384,4},{388,8},{392,12},{396,16},{400,20},{404,24},{408,2... | collective-permute-start | bytes 1966088 | tf_op jit(solution)/shard_map/ppermute | solution.py:10
  143.2 182.4 %collective-permute-start.12 = (bf16[160,2048]{1,0:T(8,128)(2,1)S(1)}, bf16[160,2048]{1,0:T(8,128)(2,1)S(1)}, u32[]{:S(2)}, u32[]{:S(2)}) collective-permute-start(bf16[160,2048]{1,0:T(8,128)(2,1)S(1)} %bitcast.328), channel_id=1, source_target_pairs={{128,0},{132,4},{136,8},{140,12},{144,16},{148,20},{152,24},{156,2... | collective-permute-start | bytes 1966088 | tf_op jit(solution)/shard_map/ppermute | solution.py:10
  147.5 245.0 %collective-permute-start.13 = (bf16[160,2048]{1,0:T(8,128)(2,1)S(1)}, bf16[160,2048]{1,0:T(8,128)(2,1)S(1)}, u32[]{:S(2)}, u32[]{:S(2)}) collective-permute-start(bf16[160,2048]{1,0:T(8,128)(2,1)S(1)} %bitcast.327), channel_id=1, source_target_pairs={{384,0},{388,4},{392,8},{396,12},{400,16},{404,20},{408,24},{412,2... | collective-permute-start | bytes 1966088 | tf_op jit(solution)/shard_map/ppermute | solution.py:10
  154.1 172.9 %copy-start.2 = (f32[16,20,8,128]{3,2,1,0:T(8,128)S(1)}, f32[16,20,8,128]{3,2,1,0:T(8,128)}, u32[]{:S(2)}) copy-start(f32[16,20,8,128]{3,2,1,0:T(8,128)} %fusion.6) | copy-start | bytes 3932164
  323.0 70.8 %collective-permute-start.11 = (bf16[160,2048]{1,0:T(8,128)(2,1)S(1)}, bf16[160,2048]{1,0:T(8,128)(2,1)S(1)}, u32[]{:S(2)}, u32[]{:S(2)}) collective-permute-start(bf16[160,2048]{1,0:T(8,128)(2,1)S(1)} %bitcast.329), channel_id=1, source_target_pairs={{380,0},{384,4},{388,8},{392,12},{396,16},{400,20},{404,24},{408,2... | collective-permute-start | bytes 1966088 | tf_op jit(solution)/shard_map/ppermute | solution.py:10
  324.3 90.4 %collective-permute-start.8 = (bf16[160,2048]{1,0:T(8,128)(2,1)S(1)}, bf16[160,2048]{1,0:T(8,128)(2,1)S(1)}, u32[]{:S(2)}, u32[]{:S(2)}) collective-permute-start(bf16[160,2048]{1,0:T(8,128)(2,1)S(1)} %bitcast.330), channel_id=1, source_target_pairs={{128,0},{132,4},{136,8},{140,12},{144,16},{148,20},{152,24},{156,2... | collective-permute-start | bytes 1966088 | tf_op jit(solution)/shard_map/ppermute | solution.py:10
  325.6 66.9 %copy-start.4 = (f32[16,20,8,128]{3,2,1,0:T(8,128)S(1)}, f32[16,20,8,128]{3,2,1,0:T(8,128)}, u32[]{:S(2)}) copy-start(f32[16,20,8,128]{3,2,1,0:T(8,128)} %convolution_bitcast_fusion) | copy-start | bytes 3932164
  325.6 228.5 %collective-permute-start.9 = (bf16[160,2048]{1,0:T(8,128)(2,1)S(1)}, bf16[160,2048]{1,0:T(8,128)(2,1)S(1)}, u32[]{:S(2)}, u32[]{:S(2)}) collective-permute-start(bf16[160,2048]{1,0:T(8,128)(2,1)S(1)} %bitcast.331), channel_id=1, source_target_pairs={{384,0},{388,4},{392,8},{396,12},{400,16},{404,20},{408,24},{412,2... | collective-permute-start | bytes 1966088 | tf_op jit(solution)/shard_map/ppermute | solution.py:10
where the time goes:
time: 556 us; the launch traced here: 555 us
  waiting for transfers between devices  473 us (85%)
  starting transfers between devices  42 us (8%)
  matrix products  32.8 us (6%)
    ppermute x16, waiting for transfers between devices, from_behind(): return lax.ppermute(shard, axis, pairs)  473 us
    ppermute x16, starting transfers between devices, from_behind(): return lax.ppermute(shard, axis, pairs)  42 us
    dot_general x5, matrix products, block_terms(): jnp.einsum('shd,thd->hst', g_heads, v_heads, preferred_element_type=jnp.f...  11.1 us
  transfers between devices with their start and end apart: 16, of which 7 were waited for; matrix products, arithmetic and copies ran while one was open for 7% of the time, Pallas kernels for 0%

commit v1 on v0

v1 whole, which is shorter than its diff:
```python
import functools

import jax
import jax.numpy as jnp
from jax import lax
from jax.experimental import pallas as pl
from jax.experimental.pallas import tpu as pltpu
from jax.sharding import PartitionSpec as P

HEADS = 16
DEPTH = 128
ROWS = 160
HALF = 80
AUX = 16
LAYER = 16
SCALE = DEPTH ** (-0.5)
NT = (((1,), (1,)), ((), ()))
NN = (((1,), (0,)), ((), ()))
TN = (((0,), (0,)), ((), ()))
VMEM_LIMIT = 48 * 1024 * 1024


def dot(a, b, dims):
    return lax.dot_general(a, b, dims, preferred_element_type=jnp.float32)


def params():
    return pltpu.CompilerParams(vmem_limit_bytes=VMEM_LIMIT)


def pair(k, v, q, g, lse, delta, mask=None):
    prob = jnp.exp(dot(k, q, NT) * SCALE - lse)
    if mask is not None:
        prob = jnp.where(mask, prob, 0.0)
    dscore = (prob * (dot(v, g, NT) - delta)).astype(jnp.bfloat16)
    prob = prob.astype(jnp.bfloat16)
    return dot(dscore, q, NN), dot(prob, g, NN), dot(dscore, k, TN)


def read_aux(aux):
    a = aux.astype(jnp.float32)
    rows = []
    for base in (0, 6):
        first = a[base : base + 1] + a[base + 2 : base + 3] + a[base + 4 : base + 5]
        second = a[base + 1 : base + 2] + a[base + 3 : base + 4] + a[base + 5 : base + 6]
        rows.append(jnp.concatenate([first, second[:, : ROWS - DEPTH]], axis=1))
    return rows


def prep_kernel(roles, q, g, k, v, lse, delta, send_a, send_b, local, wide):
    group = pl.program_id(0)
    count = send_a.shape[0]
    wide[...] = jnp.zeros_like(wide)
    wide[0, :, 0:ROWS] = lse[...]
    wide[1, :, 0:ROWS] = delta[...]
    sub = lax.broadcasted_iota(jnp.int32, (AUX, DEPTH), 0)
    for i in range(count):
        head = group * count + i
        aux = jnp.zeros((AUX, DEPTH), jnp.float32)
        for t in range(2):
            row = wide[t, pl.ds(head, 1), :]
            for piece in range(3):
                part = row.astype(jnp.bfloat16).astype(jnp.float32)
                row = row - part
                for side in range(2):
                    at = 6 * t + 2 * piece + side
                    aux = jnp.where(sub == at, part[:, side * DEPTH : (side + 1) * DEPTH], aux)
        aux = aux.astype(jnp.bfloat16)
        cols = slice(i * DEPTH, (i + 1) * DEPTH)
        send_a[i, 2 * HALF :, :] = aux
        local[i, 2 * ROWS :, :] = aux

        def put_send(one, two):
            send_a[i, 0:HALF, :] = one[0:HALF, cols]
            send_a[i, HALF : 2 * HALF, :] = two[0:HALF, cols]
            send_b[i, 0:HALF, :] = one[HALF:, cols]
            send_b[i, HALF : 2 * HALF, :] = two[HALF:, cols]

        def put_local(one, two):
            local[i, 0:ROWS, :] = one[:, cols]
            local[i, ROWS : 2 * ROWS, :] = two[:, cols]

        pl.when(roles[0] == 1)(functools.partial(put_send, q, g))
        pl.when(roles[0] == 0)(functools.partial(put_send, k, v))
        pl.when(roles[1] == 1)(functools.partial(put_local, k, v))
        pl.when(roles[1] == 0)(functools.partial(put_local, q, g))


def prep(roles, q, g, k, v, lse, delta):
    count = 4
    wide = pl.BlockSpec((ROWS, count * DEPTH), lambda i: (0, i))
    small = pl.BlockSpec((HEADS, ROWS), lambda i: (0, 0))
    heights = (2 * HALF + AUX, 2 * HALF, 2 * ROWS + AUX)
    return pl.pallas_call(
        prep_kernel,
        grid=(HEADS // count,),
        in_specs=[pl.BlockSpec(memory_space=pltpu.SMEM)] + [wide] * 4 + [small] * 2,
        out_specs=[pl.BlockSpec((count, h, DEPTH), lambda i: (i, 0, 0)) for h in heights],
        out_shape=[jax.ShapeDtypeStruct((HEADS, h, DEPTH), jnp.bfloat16) for h in heights],
        scratch_shapes=[pltpu.VMEM((2, HEADS, 2 * DEPTH), jnp.float32)],
        compiler_params=params(),
        name="prep",
    )(roles, q, g, k, v, lse, delta)


def diag_kernel(q, g, k, v, lse, delta, dq, dk, dv):
    group = pl.program_id(0)
    count = q.shape[1] // DEPTH
    mask = lax.broadcasted_iota(jnp.int32, (ROWS, ROWS), 0) <= lax.broadcasted_iota(
        jnp.int32, (ROWS, ROWS), 1
    )
    for i in range(count):
        head = group * count + i
        cols = slice(i * DEPTH, (i + 1) * DEPTH)
        key, value, query = pair(
            k[:, cols],
            v[:, cols],
            q[:, cols],
            g[:, cols],
            lse[pl.ds(head, 1), :],
            delta[pl.ds(head, 1), :],
            mask,
        )
        dq[:, cols] = query * SCALE
        dk[:, cols] = key * SCALE
        dv[:, cols] = value


def diag(q, g, k, v, lse, delta):
    count = 4
    wide = pl.BlockSpec((ROWS, count * DEPTH), lambda i: (0, i))
    small = pl.BlockSpec((HEADS, ROWS), lambda i: (0, 0))
    return pl.pallas_call(
        diag_kernel,
        grid=(HEADS // count,),
        in_specs=[wide] * 4 + [small] * 2,
        out_specs=[wide] * 3,
        out_shape=[jax.ShapeDtypeStruct((ROWS, HEADS * DEPTH), jnp.float32)] * 3,
        compiler_params=params(),
        name="diagonal",
    )(q, g, k, v, lse, delta)


def edges_kernel(first, roles, *refs):
    if first:
        recv, aux_from, local, back, acc_out = refs
    else:
        recv, aux_from, local, acc_in, back, acc_out = refs
    lanes = slice(0, HALF) if first else slice(HALF, ROWS)
    if not first:
        acc_out[...] = acc_in[...]

    def block(i, lo, count, role_b):
        r1 = recv[i, 0:HALF, :]
        r2 = recv[i, HALF : 2 * HALF, :]
        l1 = [local[lo + c, 0:ROWS, :] for c in range(count)]
        l2 = [local[lo + c, ROWS : 2 * ROWS, :] for c in range(count)]
        l1 = jnp.concatenate(l1, axis=0)
        l2 = jnp.concatenate(l2, axis=0)
        if role_b:
            lse, delta = [x[:, lanes] for x in read_aux(aux_from[i, 2 * HALF :, :])]
            key, value, query = pair(l1, l2, r1, r2, lse, delta)
            back[i, 0:HALF, :] = (query * SCALE).astype(jnp.bfloat16)
            back[i, HALF : 2 * HALF, :] = jnp.zeros((HALF, DEPTH), jnp.bfloat16)
            sums = (key, value)
        else:
            aux = [read_aux(local[lo + c, 2 * ROWS :, :]) for c in range(count)]
            lse = jnp.concatenate([a[0] for a in aux], axis=1)
            delta = jnp.concatenate([a[1] for a in aux], axis=1)
            key, value, query = pair(r1, r2, l1, l2, lse, delta)
            back[i, 0:HALF, :] = (key * SCALE).astype(jnp.bfloat16)
            back[i, HALF : 2 * HALF, :] = value.astype(jnp.bfloat16)
            sums = (query,)
        for n, term in enumerate(sums):
            if count == 2 or not first:
                acc_out[n, lo] += term[0:ROWS]
            else:
                acc_out[n, lo] = term[0:ROWS]
            if count == 2:
                if first:
                    acc_out[n, lo + 1] = term[ROWS:]
                else:
                    acc_out[n, lo + 1] += term[ROWS:]

    def run(role_b):
        block(0, 0, 1, role_b)

        @pl.loop(1, LAYER)
        def _(i):
            block(i, i - 1, 2, role_b)

        if first and not role_b:
            acc_out[1] = jnp.zeros(acc_out.shape[1:], jnp.float32)

    pl.when(roles[1] == 1)(functools.partial(run, True))
    pl.when(roles[1] == 0)(functools.partial(run, False))


def edges(first, roles, recv, aux_from, local, acc):
    vmem = pl.BlockSpec(memory_space=pltpu.VMEM)
    ops = [recv, aux_from, local] + ([] if first else [acc])
    sums = jax.ShapeDtypeStruct((2, LAYER, ROWS, DEPTH), jnp.float32)
    return pl.pallas_call(
        functools.partial(edges_kernel, first),
        in_specs=[pl.BlockSpec(memory_space=pltpu.SMEM)] + [vmem] * len(ops),
        out_specs=[vmem] * 2,
        out_shape=[jax.ShapeDtypeStruct((LAYER, 2 * HALF, DEPTH), jnp.bfloat16), sums],
        input_output_aliases={} if first else {4: 1},
        compiler_params=params(),
        name="edges_first" if first else "edges_second",
    )(roles, *ops)


def carry_kernel(roles, chain, extra, local, acc, back, mine, out):
    layer = roles[2]
    out[:, 0:ROWS, :] = (acc[0] * SCALE).astype(jnp.bfloat16)
    out[:, ROWS : 2 * ROWS, :] = acc[1].astype(jnp.bfloat16)
    last = LAYER - 1
    recv = jnp.where(layer == 7, extra[...], chain[...])
    held = jnp.where(layer == 5, extra[...], local[last])
    r1, r2, l1, l2 = recv[0:ROWS], recv[ROWS : 2 * ROWS], held[0:ROWS], held[ROWS : 2 * ROWS]

    @pl.when(layer <= 4)
    def _():
        lse, delta = read_aux(recv[2 * ROWS :])
        key, value, query = pair(l1, l2, r1, r2, lse, delta)
        back[0:ROWS, :] = (query * SCALE).astype(jnp.bfloat16)
        back[ROWS:, :] = jnp.zeros((ROWS, DEPTH), jnp.bfloat16)
        out[last, 0:ROWS, :] = ((acc[0, last] + key) * SCALE).astype(jnp.bfloat16)
        out[last, ROWS : 2 * ROWS, :] = (acc[1, last] + value).astype(jnp.bfloat16)
        mine[...] = jnp.zeros_like(mine)

    @pl.when(layer > 4)
    def _():
        lse, delta = read_aux(held[2 * ROWS :])
        key, value, query = pair(r1, r2, l1, l2, lse, delta)
        back[0:ROWS, :] = (key * SCALE).astype(jnp.bfloat16)
        back[ROWS:, :] = value.astype(jnp.bfloat16)
        mine[...] = (query * SCALE).astype(jnp.bfloat16)


def carry(roles, chain, extra, local, acc):
    vmem = pl.BlockSpec(memory_space=pltpu.VMEM)
    return pl.pallas_call(
        carry_kernel,
        in_specs=[pl.BlockSpec(memory_space=pltpu.SMEM)] + [vmem] * 4,
        out_specs=[vmem] * 3,
        out_shape=[
            jax.ShapeDtypeStruct((2 * ROWS, DEPTH), jnp.bfloat16),
            jax.ShapeDtypeStruct((ROWS, DEPTH), jnp.bfloat16),
            jax.ShapeDtypeStruct((LAYER, 2 * ROWS, DEPTH), jnp.bfloat16),
        ],
        compiler_params=params(),
        name="carry",
    )(roles, chain, extra, local, acc)


def final_kernel(roles, dq, dk, dv, one, two, own, oq, ok, ov):
    layer = roles[2]
    for i in range(one.shape[0]):
        cols = slice(i * DEPTH, (i + 1) * DEPTH)
        own1 = own[i, 0:ROWS, :].astype(jnp.float32)
        own2 = own[i, ROWS : 2 * ROWS, :].astype(jnp.float32)
        a1 = one[i, 0:HALF, :].astype(jnp.float32)
        a2 = one[i, HALF : 2 * HALF, :].astype(jnp.float32)
        b1 = two[i, 0:HALF, :].astype(jnp.float32)
        b2 = two[i, HALF : 2 * HALF, :].astype(jnp.float32)

        def put(query, key, value):
            oq[:, cols] = query.astype(jnp.bfloat16)
            ok[:, cols] = key.astype(jnp.bfloat16)
            ov[:, cols] = value.astype(jnp.bfloat16)

        @pl.when(layer <= 1)
        def _():
            put(
                dq[:, cols],
                dk[:, cols] + own1 + jnp.concatenate([a1, b1], axis=0),
                dv[:, cols] + own2 + jnp.concatenate([a2, b2], axis=0),
            )

        @pl.when(jnp.logical_and(layer >= 2, layer <= 5))
        def _():
            put(
                dq[:, cols] + jnp.concatenate([a1, b1 + a2], axis=0),
                dk[:, cols] + own1,
                dv[:, cols] + own2,
            )

        @pl.when(layer >= 6)
        def _():
            put(
                dq[:, cols] + own1 + jnp.concatenate([a1, b1 + a2], axis=0),
                dk[:, cols],
                dv[:, cols],
            )


def final(roles, dq, dk, dv, one, two, own):
    count = 4
    wide = pl.BlockSpec((ROWS, count * DEPTH), lambda i: (0, i))
    head = [pl.BlockSpec((count, x.shape[1], DEPTH), lambda i: (i, 0, 0)) for x in (one, two, own)]
    return pl.pallas_call(
        final_kernel,
        grid=(HEADS // count,),
        in_specs=[pl.BlockSpec(memory_space=pltpu.SMEM)] + [wide] * 3 + head,
        out_specs=[wide] * 3,
        out_shape=[jax.ShapeDtypeStruct((ROWS, HEADS * DEPTH), jnp.bfloat16)] * 3,
        compiler_params=params(),
        name="final",
    )(roles, dq, dk, dv, one, two, own)


def after(x, *others):
    return lax.optimization_barrier((x, *others))[0]


def on_device(queries, keys, values, out_grad, log_sum, delta):
    count = lax.axis_size("seq")
    position = lax.axis_index("seq")
    layer = position // LAYER
    groups = [list(range(s, s + LAYER)) for s in range(0, count, LAYER)]

    def ring(x, by):
        return lax.ppermute(x, "seq", [(i, (i + by) % count) for i in range(count)])

    def spread(x):
        return lax.all_to_all(x, "seq", 0, 0, axis_index_groups=groups, tiled=True)

    roles = jnp.stack([layer >= 2, layer <= 5, layer, layer]).astype(jnp.int32)
    send_a, send_b, local = prep(roles, queries, out_grad, keys, values, log_sum, delta)
    recv_a = ring(send_a, -2 * LAYER)
    head_b = spread(send_b)
    recv_b = ring(head_b, -2 * LAYER)
    head_local = spread(after(local, head_b))
    dq, dk, dv = diag(queries, out_grad, keys, values, after(log_sum, head_local), delta)
    recv_a = spread(recv_a)
    back_a, acc = edges(True, roles, recv_a, recv_a, head_local, None)
    home_a = ring(back_a, 2 * LAYER)
    back_b, acc = edges(False, roles, after(recv_b, back_a), recv_a, head_local, acc)
    back_b = spread(back_b)
    home_b = ring(back_b, 2 * LAYER)

    def whole(block):
        a, b = recv_a[block], recv_b[block]
        return jnp.concatenate(
            [a[0:HALF], b[0:HALF], a[HALF : 2 * HALF], b[HALF : 2 * HALF], a[2 * HALF :]], axis=0
        )

    chain = lax.ppermute(whole(0), "seq", [(i, i - LAYER) for i in range(LAYER, count)])
    extra = jnp.where(layer == 2, head_local[0], whole(LAYER - 1))
    extra = lax.ppermute(
        extra,
        "seq",
        [(2 * LAYER + i, 7 * LAYER + i) for i in range(LAYER)]
        + [(3 * LAYER + i, 5 * LAYER + i) for i in range(LAYER)],
    )
    carry_back, carry_mine, own = carry(roles, chain, extra, head_local, acc)
    carry_home = ring(carry_back, 3 * LAYER)
    zero = jnp.bfloat16(0.0)
    own = own.at[0].add(jnp.where(layer <= 2, carry_home, zero))
    own = spread(own)
    from_home = jnp.where(layer >= 3, carry_home[0:ROWS], zero)
    from_mine = jnp.where(layer >= 5, carry_mine, zero)
    home_a = home_a.at[0].add(from_home).at[LAYER - 1].add(from_mine)
    home_a = spread(after(home_a, own))
    return final(roles, dq, dk, dv, home_a, home_b, own)


def solution(mesh):
    rows = P(("grp", "seq"), None)
    cols = P(None, ("grp", "seq"))
    return jax.shard_map(
        on_device,
        mesh=mesh,
        in_specs=(rows, rows, rows, rows, cols, cols),
        out_specs=(rows, rows, rows),
        check_vma=False,
    )
```

time: 556 us -> 231 us (0.42)
  the two profiles are of different devices: /device:TPU:22 before, /device:TPU:8 now
where the time goes in v1:
time: 231 us; the launch traced here: 229 us
  starting transfers between devices  82.8 us (36%)
  waiting for transfers between devices  72.7 us (31%)
  Pallas kernels  30.7 us (13%)
  local copies, waits for them, and re-layouts  19.7 us (9%)
  blocking collectives  18.2 us (8%)
  other arithmetic  4.47 us (2%)
    ppermute x5, waiting for transfers between devices, ring(): return lax.ppermute(x, 'seq', [(i, (i + by) % count) for i in range(count)])  59.7 us
    ppermute x5, starting transfers between devices, ring(): return lax.ppermute(x, 'seq', [(i, (i + by) % count) for i in range(count)])  49 us
    all_to_all x5, starting transfers between devices, spread(): return lax.all_to_all(x, 'seq', 0, 0, axis_index_groups=groups, tiled=True)  31.8 us
    unnamed x48, local copies, waits for them, and re-layouts  19.1 us
    all_to_all x1, blocking collectives, spread(): return lax.all_to_all(x, 'seq', 0, 0, axis_index_groups=groups, tiled=True)  18.2 us
    pallas_call x2, Pallas kernels, edges(): pl.pallas_call(functools.partial(edges_kernel, first), in_specs=[pl.Block...  14.9 us
    all_to_all x5, waiting for transfers between devices, spread(): return lax.all_to_all(x, 'seq', 0, 0, axis_index_groups=groups, tiled=True)  13 us
    pallas_call x1, Pallas kernels, diag(): pl.pallas_call(diag_kernel, grid=(HEADS // count,), in_specs=[wide] * 4 +...  6.2 us
  transfers between devices with their start and end apart: 12, of which 7 were waited for; matrix products, arithmetic and copies ran while one was open for 3% of the time, Pallas kernels for 10%

profile of v1, /device:TPU:8, one launch (start us, length us, event | category | flops | bytes accessed | tf_op | source)
XLA Modules:
  0.0 229.4 jit_solution(14029896387733498432)
XLA Ops:
  6.5 3.0 %prep.1 = (bf16[16,176,128]{2,1,0:T(8,128)(2,1)S(1)}, bf16[16,160,128]{2,1,0:T(8,128)(2,1)S(1)}, bf16[16,336,128]{2,1,0:T(8,128)(2,1)}) custom-call(s32[4]{0:T(128)S(1)} %pad_add_fusion.roles, bf16[160,2048]{1,0:T(8,128)(2,1)S(1)} %copy-done.2, bf16[160,2048]{1,0:T(8,128)(2,1)S(1)} %copy-done.4, bf16[160,2048]{1,0:T(8,128)(2,1)S(1)} %copy-done.6, ...), custom_call_target="tpu_custom_call" | custom-call | tf_op jit(solution)/shard_map/prep/pallas_call | solution.py:94
  9.5 11.7 %collective-permute-start = (bf16[16,176,128]{2,1,0:T(8,128)(2,1)S(1)}, bf16[16,176,128]{2,1,0:T(8,128)(2,1)}, u32[]{:S(2)}, u32[]{:S(2)}) collective-permute-start(bf16[16,176,128]{2,1,0:T(8,128)(2,1)S(1)} %get-tuple-element.63), channel_id=1, source_target_pairs={{0,384},{4,388},{8,392},{12,396},{16,400},{20,404},{24,408},{28,41... | collective-permute-start | bytes 2162696 | tf_op jit(solution)/shard_map/ppermute | solution.py:325
  21.2 18.2 %all_to_all.30 = bf16[16,160,128]{2,1,0:T(8,128)(2,1)S(1)} all-to-all(bf16[16,160,128]{2,1,0:T(8,128)(2,1)S(1)} %get-tuple-element.57), channel_id=1, replica_groups={{0,4,8,12,16,20,24,28,32,36,40,44,48,52,56,60},{64,68,72,76,80,84,88,92..., dimensions={0} | all-to-all | bytes 1310720 | tf_op jit(solution)/shard_map/all_to_all | solution.py:328
  39.4 6.8 %collective-permute-done = bf16[16,176,128]{2,1,0:T(8,128)(2,1)} collective-permute-done((bf16[16,176,128]{2,1,0:T(8,128)(2,1)S(1)}, bf16[16,176,128]{2,1,0:T(8,128)(2,1)}, u32[]{:S(2)}, u32[]{:S(2)}) %collective-permute-start) | collective-permute-done | bytes 720928 | tf_op jit(solution)/shard_map/ppermute | solution.py:325
  46.3 7.4 %all-to-all-start.2 = ((bf16[16,176,128]{2,1,0:T(8,128)(2,1)}), bf16[16,176,128]{2,1,0:T(8,128)(2,1)S(1)}, u32[]{:S(2)}, u32[]{:S(2)}) async-start(bf16[16,176,128]{2,1,0:T(8,128)(2,1)} %collective-permute-done), calls=%async_computation.2 | async-start | bytes 1441792 | tf_op jit(solution)/shard_map/all_to_all | solution.py:328
  53.7 8.0 %collective-permute-start.2 = (bf16[16,160,128]{2,1,0:T(8,128)(2,1)S(1)}, bf16[16,160,128]{2,1,0:T(8,128)(2,1)S(1)}, u32[]{:S(2)}, u32[]{:S(2)}) collective-permute-start(bf16[16,160,128]{2,1,0:T(8,128)(2,1)S(1)} %all_to_all.30), channel_id=1, source_target_pairs={{0,384},{4,388},{8,392},{12,396},{16,400},{20,404},{24,408},{28,41... | collective-permute-start | bytes 1966088 | tf_op jit(solution)/shard_map/ppermute | solution.py:325
  61.7 3.6 %all-to-all-done.2.refs_0_.refs_1_ = bf16[16,176,128]{2,1,0:T(8,128)(2,1)S(1)} async-done(((bf16[16,176,128]{2,1,0:T(8,128)(2,1)}), bf16[16,176,128]{2,1,0:T(8,128)(2,1)S(1)}, u32[]{:S(2)}, u32[]{:S(2)}) %all-to-all-start.2) | async-done | bytes 720928 | tf_op jit(solution)/shard_map/all_to_all | solution.py:328
  65.4 5.0 %all-to-all-start.1 = ((bf16[16,336,128]{2,1,0:T(8,128)(2,1)}), bf16[16,336,128]{2,1,0:T(8,128)(2,1)S(1)}, u32[]{:S(2)}, u32[]{:S(2)}) async-start(bf16[16,336,128]{2,1,0:T(8,128)(2,1)} %get-tuple-element.58), calls=%async_computation.1 | async-start | bytes 2752512 | tf_op jit(solution)/shard_map/all_to_all | solution.py:328
  70.9 5.2 %collective-permute-done.2.refs_0_ = bf16[16,160,128]{2,1,0:T(8,128)(2,1)S(1)} collective-permute-done((bf16[16,160,128]{2,1,0:T(8,128)(2,1)S(1)}, bf16[16,160,128]{2,1,0:T(8,128)(2,1)S(1)}, u32[]{:S(2)}, u32[]{:S(2)}) %collective-permute-start.2) | collective-permute-done | bytes 655392 | tf_op jit(solution)/shard_map/ppermute | solution.py:325
  79.1 1.3 collective-permute-start.3
  80.4 8.3 %all-to-all-done.1.refs_2_.local = bf16[16,336,128]{2,1,0:T(8,128)(2,1)S(1)} async-done(((bf16[16,336,128]{2,1,0:T(8,128)(2,1)}), bf16[16,336,128]{2,1,0:T(8,128)(2,1)S(1)}, u32[]{:S(2)}, u32[]{:S(2)}) %all-to-all-start.1) | async-done | bytes 1376288 | tf_op jit(solution)/shard_map/all_to_all | solution.py:328
  88.8 6.9 %edges_first.1 = (bf16[16,160,128]{2,1,0:T(8,128)(2,1)S(1)}, f32[2,16,160,128]{3,2,1,0:T(8,128)S(1)}) custom-call(s32[4]{0:T(128)S(1)} %pad_add_fusion.roles, bf16[16,176,128]{2,1,0:T(8,128)(2,1)S(1)} %all-to-all-done.2.refs_0_.refs_1_, bf16[16,176,128]{2,1,0:T(8,128)(2,1)S(1)} %all-to-all-done.2.refs_0_.refs_1_, ...), custom_call_target="tpu_custom_call" | custom-call | tf_op jit(solution)/shard_map/edges_first/pallas_call | solution.py:203
  95.7 8.0 %edges_second.1 = (bf16[16,160,128]{2,1,0:T(8,128)(2,1)}, f32[2,16,160,128]{3,2,1,0:T(8,128)S(1)}) custom-call(s32[4]{0:T(128)S(1)} %pad_add_fusion.roles, bf16[16,160,128]{2,1,0:T(8,128)(2,1)S(1)} %collective-permute-done.2.refs_0_, bf16[16,176,128]{2,1,0:T(8,128)(2,1)S(1)} %all-to-all-done.2.refs_0_.refs_1_, ...), custom_call_target="tpu_custom_call", output_to_operand_aliasing={{1}: (4, {})} | custom-call | tf_op jit(solution)/shard_map/edges_second/pallas_call | solution.py:203
  103.7 1.5 copy-done
  105.2 5.0 %all-to-all-start.5 = ((bf16[16,160,128]{2,1,0:T(8,128)(2,1)}), bf16[16,160,128]{2,1,0:T(8,128)(2,1)S(1)}, u32[]{:S(2)}, u32[]{:S(2)}) async-start(bf16[16,160,128]{2,1,0:T(8,128)(2,1)} %get-tuple-element.72), calls=%async_computation.5 | async-start | bytes 1310720 | tf_op jit(solution)/shard_map/all_to_all | solution.py:328
  110.9 1.7 copy-done.1
  112.7 2.2 carry.1
  114.9 19.0 %collective-permute-start.5 = (bf16[320,128]{1,0:T(8,128)(2,1)S(1)}, bf16[320,128]{1,0:T(8,128)(2,1)S(1)}, u32[]{:S(2)}, u32[]{:S(2)}) collective-permute-start(bf16[320,128]{1,0:T(8,128)(2,1)S(1)} %get-tuple-element.68), channel_id=1, source_target_pairs={{0,192},{4,196},{8,200},{12,204},{16,208},{20,212},{24,216},{28,22... | collective-permute-start | bytes 245768 | tf_op jit(solution)/shard_map/ppermute | solution.py:325
  133.9 6.3 %collective-permute-done.5 = bf16[320,128]{1,0:T(8,128)(2,1)S(1)} collective-permute-done((bf16[320,128]{1,0:T(8,128)(2,1)S(1)}, bf16[320,128]{1,0:T(8,128)(2,1)S(1)}, u32[]{:S(2)}, u32[]{:S(2)}) %collective-permute-start.5) | collective-permute-done | bytes 81952 | tf_op jit(solution)/shard_map/ppermute | solution.py:325
  140.2 1.5 fusion.1
  142.6 7.2 %all-to-all-start.3 = ((bf16[16,320,128]{2,1,0:T(8,128)(2,1)}), bf16[16,320,128]{2,1,0:T(8,128)(2,1)}, u32[]{:S(2)}, u32[]{:S(2)}) async-start(bf16[16,320,128]{2,1,0:T(8,128)(2,1)} %fusion.1), calls=%async_computation.3 | async-start | bytes 2621440 | tf_op jit(solution)/shard_map/all_to_all | solution.py:328
  149.9 8.2 %collective-permute-start.1 = (bf16[16,160,128]{2,1,0:T(8,128)(2,1)S(1)}, bf16[16,160,128]{2,1,0:T(8,128)(2,1)}, u32[]{:S(2)}, u32[]{:S(2)}) collective-permute-start(bf16[16,160,128]{2,1,0:T(8,128)(2,1)S(1)} %get-tuple-element.64), channel_id=1, source_target_pairs={{0,128},{4,132},{8,136},{12,140},{16,144},{20,148},{24,152},{28,15... | collective-permute-start | bytes 1966088 | tf_op jit(solution)/shard_map/ppermute | solution.py:325
  158.1 2.1 collective-permute-start.6
  160.2 41.4 %collective-permute-done.1 = bf16[16,160,128]{2,1,0:T(8,128)(2,1)} collective-permute-done((bf16[16,160,128]{2,1,0:T(8,128)(2,1)S(1)}, bf16[16,160,128]{2,1,0:T(8,128)(2,1)}, u32[]{:S(2)}, u32[]{:S(2)}) %collective-permute-start.1) | collective-permute-done | bytes 655392 | tf_op jit(solution)/shard_map/ppermute | solution.py:325
  201.6 1.4 fusion.5
  203.0 1.4 fusion.2
  204.4 7.2 %all-to-all-start.4 = ((bf16[16,160,128]{2,1,0:T(8,128)(2,1)}), bf16[16,160,128]{2,1,0:T(8,128)(2,1)S(1)}, u32[]{:S(2)}, u32[]{:S(2)}) async-start(bf16[16,160,128]{2,1,0:T(8,128)(2,1)} %fusion.2), calls=%async_computation.4 | async-start | bytes 1310720 | tf_op jit(solution)/shard_map/all_to_all | solution.py:328
  211.7 6.2 %diagonal.1 = (f32[160,2048]{1,0:T(8,128)S(1)}, f32[160,2048]{1,0:T(8,128)S(1)}, f32[160,2048]{1,0:T(8,128)}) custom-call(bf16[160,2048]{1,0:T(8,128)(2,1)S(1)} %copy-done.3, bf16[160,2048]{1,0:T(8,128)(2,1)S(1)} %copy-done.5, bf16[160,2048]{1,0:T(8,128)(2,1)S(1)} %copy-done.7, bf16[160,2048]{1,0:T(8,128)(2,1)S(1)} %copy-done.9, f32[16,160]{1,0:T(8,128)S(1)} %copy-done.16, ...), custom_call_target="tpu_custom_call" | custom-call | tf_op jit(solution)/shard_map/diagonal/pallas_call | solution.py:133
  221.1 1.3 copy-done.11
  222.4 1.3 copy-done.13
  223.7 1.3 copy-done.14
  225.0 4.3 %final.1 = (bf16[160,2048]{1,0:T(8,128)(2,1)}, bf16[160,2048]{1,0:T(8,128)(2,1)}, bf16[160,2048]{1,0:T(8,128)(2,1)}) custom-call(s32[4]{0:T(128)S(1)} %pad_add_fusion.roles, f32[160,2048]{1,0:T(8,128)S(1)} %copy-done.11, f32[160,2048]{1,0:T(8,128)S(1)} %copy-done.13, f32[160,2048]{1,0:T(8,128)S(1)} %copy-done.14, ...), custom_call_target="tpu_custom_call" | custom-call | tf_op jit(solution)/shard_map/final/pallas_call | solution.py:303
  (53 shorter events, 14.3 us)
Async XLA Ops:
  0.7 1.1 copy-start.2
  1.8 1.1 copy-start.4
  2.9 1.1 copy-start.6
  4.0 1.1 copy-start.8
  5.1 0.7 copy-start.15
  9.5 36.7 %collective-permute-start = (bf16[16,176,128]{2,1,0:T(8,128)(2,1)S(1)}, bf16[16,176,128]{2,1,0:T(8,128)(2,1)}, u32[]{:S(2)}, u32[]{:S(2)}) collective-permute-start(bf16[16,176,128]{2,1,0:T(8,128)(2,1)S(1)} %get-tuple-element.63), channel_id=1, source_target_pairs={{0,384},{4,388},{8,392},{12,396},{16,400},{20,404},{24,408},{28,41... | collective-permute-start | bytes 2162696 | tf_op jit(solution)/shard_map/ppermute | solution.py:325
  46.3 19.1 %all-to-all-start.2 = ((bf16[16,176,128]{2,1,0:T(8,128)(2,1)}), bf16[16,176,128]{2,1,0:T(8,128)(2,1)S(1)}, u32[]{:S(2)}, u32[]{:S(2)}) async-start(bf16[16,176,128]{2,1,0:T(8,128)(2,1)} %collective-permute-done), calls=%async_computation.2 | async-start | bytes 1441792 | tf_op jit(solution)/shard_map/all_to_all | solution.py:328
  53.7 22.4 %collective-permute-start.2 = (bf16[16,160,128]{2,1,0:T(8,128)(2,1)S(1)}, bf16[16,160,128]{2,1,0:T(8,128)(2,1)S(1)}, u32[]{:S(2)}, u32[]{:S(2)}) collective-permute-start(bf16[16,160,128]{2,1,0:T(8,128)(2,1)S(1)} %all_to_all.30), channel_id=1, source_target_pairs={{0,384},{4,388},{8,392},{12,396},{16,400},{20,404},{24,408},{28,41... | collective-permute-start | bytes 1966088 | tf_op jit(solution)/shard_map/ppermute | solution.py:325
  65.4 23.4 %all-to-all-start.1 = ((bf16[16,336,128]{2,1,0:T(8,128)(2,1)}), bf16[16,336,128]{2,1,0:T(8,128)(2,1)S(1)}, u32[]{:S(2)}, u32[]{:S(2)}) async-start(bf16[16,336,128]{2,1,0:T(8,128)(2,1)} %get-tuple-element.58), calls=%async_computation.1 | async-start | bytes 2752512 | tf_op jit(solution)/shard_map/all_to_all | solution.py:328
  79.1 31.8 %collective-permute-start.3 = (bf16[336,128]{1,0:T(8,128)(2,1)}, bf16[336,128]{1,0:T(8,128)(2,1)S(1)}, u32[]{:S(2)}, u32[]{:S(2)}) collective-permute-start(bf16[336,128]{1,0:T(8,128)(2,1)} %get-tuple-element.74), channel_id=1, source_target_pairs={{64,0},{68,4},{72,8},{76,12},{80,16},{84,20},{88,24},{92,28},{96,3... | collective-permute-start | bytes 258056 | tf_op jit(solution)/shard_map/ppermute | solution.py:350
  103.7 1.5 copy-start
  105.2 5.0 %copy-start.21 = (bf16[336,128]{1,0:T(8,128)(2,1)S(1)}, bf16[336,128]{1,0:T(8,128)(2,1)}, u32[]{:S(2)}) copy-start(bf16[336,128]{1,0:T(8,128)(2,1)} %copy-done.20) | copy-start | bytes 258052
  105.2 36.6 %all-to-all-start.5 = ((bf16[16,160,128]{2,1,0:T(8,128)(2,1)}), bf16[16,160,128]{2,1,0:T(8,128)(2,1)S(1)}, u32[]{:S(2)}, u32[]{:S(2)}) async-start(bf16[16,160,128]{2,1,0:T(8,128)(2,1)} %get-tuple-element.72), calls=%async_computation.5 | async-start | bytes 1310720 | tf_op jit(solution)/shard_map/all_to_all | solution.py:328
  110.2 0.7 collective-permute-start.4
  110.9 1.7 copy-start.1
  114.9 25.3 %collective-permute-start.5 = (bf16[320,128]{1,0:T(8,128)(2,1)S(1)}, bf16[320,128]{1,0:T(8,128)(2,1)S(1)}, u32[]{:S(2)}, u32[]{:S(2)}) collective-permute-start(bf16[320,128]{1,0:T(8,128)(2,1)S(1)} %get-tuple-element.68), channel_id=1, source_target_pairs={{0,192},{4,196},{8,200},{12,204},{16,208},{20,212},{24,216},{28,22... | collective-permute-start | bytes 245768 | tf_op jit(solution)/shard_map/ppermute | solution.py:325
  141.8 0.8 copy-start.19
  141.8 69.9 %copy-start.7 = (bf16[160,2048]{1,0:T(8,128)(2,1)S(1)}, bf16[160,2048]{1,0:T(8,128)(2,1)}, u32[]{:S(2)}) copy-start(bf16[160,2048]{1,0:T(8,128)(2,1)} %k.3) | copy-start | bytes 1966084
  141.8 69.9 %copy-start.9 = (bf16[160,2048]{1,0:T(8,128)(2,1)S(1)}, bf16[160,2048]{1,0:T(8,128)(2,1)}, u32[]{:S(2)}) copy-start(bf16[160,2048]{1,0:T(8,128)(2,1)} %v.3) | copy-start | bytes 1966084
  142.6 61.8 %all-to-all-start.3 = ((bf16[16,320,128]{2,1,0:T(8,128)(2,1)}), bf16[16,320,128]{2,1,0:T(8,128)(2,1)}, u32[]{:S(2)}, u32[]{:S(2)}) async-start(bf16[16,320,128]{2,1,0:T(8,128)(2,1)} %fusion.1), calls=%async_computation.3 | async-start | bytes 2621440 | tf_op jit(solution)/shard_map/all_to_all | solution.py:328
  149.8 61.8 %copy-start.3 = (bf16[160,2048]{1,0:T(8,128)(2,1)S(1)}, bf16[160,2048]{1,0:T(8,128)(2,1)}, u32[]{:S(2)}) copy-start(bf16[160,2048]{1,0:T(8,128)(2,1)} %q.3) | copy-start | bytes 1966084
  149.8 61.8 %copy-start.5 = (bf16[160,2048]{1,0:T(8,128)(2,1)S(1)}, bf16[160,2048]{1,0:T(8,128)(2,1)}, u32[]{:S(2)}) copy-start(bf16[160,2048]{1,0:T(8,128)(2,1)} %g.3) | copy-start | bytes 1966084
  149.8 61.8 %copy-start.16 = (f32[16,160]{1,0:T(8,128)S(1)}, f32[16,160]{1,0:T(8,128)}, u32[]{:S(2)}) copy-start(f32[16,160]{1,0:T(8,128)} %lse.2) | copy-start | bytes 30724
  149.9 61.8 %copy-start.18 = (f32[16,160]{1,0:T(8,128)S(1)}, f32[16,160]{1,0:T(8,128)}, u32[]{:S(2)}) copy-start(f32[16,160]{1,0:T(8,128)} %delta.3) | copy-start | bytes 30724
  149.9 51.7 %collective-permute-start.1 = (bf16[16,160,128]{2,1,0:T(8,128)(2,1)S(1)}, bf16[16,160,128]{2,1,0:T(8,128)(2,1)}, u32[]{:S(2)}, u32[]{:S(2)}) collective-permute-start(bf16[16,160,128]{2,1,0:T(8,128)(2,1)S(1)} %get-tuple-element.64), channel_id=1, source_target_pairs={{0,128},{4,132},{8,136},{12,140},{16,144},{20,148},{24,152},{28,15... | collective-permute-start | bytes 1966088 | tf_op jit(solution)/shard_map/ppermute | solution.py:325
  158.1 62.0 %collective-permute-start.6 = (bf16[16,160,128]{2,1,0:T(8,128)(2,1)}, bf16[16,160,128]{2,1,0:T(8,128)(2,1)}, u32[]{:S(2)}, u32[]{:S(2)}) collective-permute-start(bf16[16,160,128]{2,1,0:T(8,128)(2,1)} %copy-done.19), channel_id=1, source_target_pairs={{0,128},{4,132},{8,136},{12,140},{16,144},{20,148},{24,152},{28,15... | collective-permute-start | bytes 1966088 | tf_op jit(solution)/shard_map/ppermute | solution.py:325
  204.4 16.7 %all-to-all-start.4 = ((bf16[16,160,128]{2,1,0:T(8,128)(2,1)}), bf16[16,160,128]{2,1,0:T(8,128)(2,1)S(1)}, u32[]{:S(2)}, u32[]{:S(2)}) async-start(bf16[16,160,128]{2,1,0:T(8,128)(2,1)} %fusion.2), calls=%async_computation.4 | async-start | bytes 1310720 | tf_op jit(solution)/shard_map/all_to_all | solution.py:328
  217.9 1.1 copy-start.10
  219.0 1.1 copy-start.12
  221.1 1.3 copy-start.11
  222.4 1.3 copy-start.13
  223.7 1.3 copy-start.14
  (2 other events, 1.4 us)

commit v2 on v0

v2 whole, which is shorter than its diff:
```python
import functools

import jax
import jax.numpy as jnp
from jax import lax
from jax.experimental import pallas as pl
from jax.experimental.pallas import tpu as pltpu
from jax.sharding import PartitionSpec as P

HEADS = 16
DEPTH = 128
ROWS = 160
AUX = 16
SENT = 2 * ROWS + AUX
BACK = 2 * ROWS
LAYER = 16
UNIT = 2
CHUNKS = (6, 6, 4)
SCALE = DEPTH ** (-0.5)
NT = (((1,), (1,)), ((), ()))
NN = (((1,), (0,)), ((), ()))
TN = (((0,), (0,)), ((), ()))
LIMIT = 60 * 1024 * 1024


def dot(a, b, dims):
    return lax.dot_general(a, b, dims, preferred_element_type=jnp.float32)


def cost(us):
    return pl.CostEstimate(
        flops=int(us * 1.1e9) + 1000, bytes_accessed=int(us * 3.6e6) + 1000, transcendentals=0
    )


def call(body, name, grid=(), us=0, limit=LIMIT, **kwargs):
    return pl.pallas_call(
        body,
        grid=grid,
        compiler_params=pltpu.CompilerParams(vmem_limit_bytes=limit),
        cost_estimate=cost(us),
        name=name,
        **kwargs,
    )


SMEM = pl.BlockSpec(memory_space=pltpu.SMEM)
ANY = pl.BlockSpec(memory_space=pl.ANY)
SMALL = pl.BlockSpec((HEADS, ROWS), lambda i: (0, 0))


def wide(first, unit=UNIT):
    return pl.BlockSpec((ROWS, unit * DEPTH), lambda i: (0, first // unit + i))


def tall(rows, first=0, unit=UNIT):
    return pl.BlockSpec((unit, rows, DEPTH), lambda i: (first // unit + i, 0, 0))


def together(*arrays):
    return lax.optimization_barrier(arrays)


def arrived_kernel(x, out):
    del x, out


def arrived(x, *others, us=100):
    if others:
        x = together(x, *others)[0]
    return call(
        arrived_kernel,
        "arrived",
        us=us,
        in_specs=[ANY],
        out_specs=ANY,
        out_shape=jax.ShapeDtypeStruct(x.shape, x.dtype),
        input_output_aliases={0: 0},
    )(x)


def pair(k, v, q, g, lse, delta, mask=None):
    prob = jnp.exp(dot(k, q, NT) * SCALE - lse)
    if mask is not None:
        prob = jnp.where(mask, prob, 0.0)
    dscore = (prob * (dot(v, g, NT) - delta)).astype(jnp.bfloat16)
    prob = prob.astype(jnp.bfloat16)
    return dot(dscore, q, NN) * SCALE, dot(prob, g, NN), dot(dscore, k, TN) * SCALE


def aux_rows(spare, head):
    sub = lax.broadcasted_iota(jnp.int32, (AUX, DEPTH), 0)
    aux = jnp.zeros((AUX, DEPTH), jnp.float32)
    for t in range(2):
        row = spare[t, pl.ds(head, 1), :]
        for piece in range(3):
            part = row.astype(jnp.bfloat16).astype(jnp.float32)
            row = row - part
            for side in range(2):
                at = 6 * t + 2 * piece + side
                aux = jnp.where(sub == at, part[:, side * DEPTH : (side + 1) * DEPTH], aux)
    return aux.astype(jnp.bfloat16)


def read_aux(aux):
    a = aux.astype(jnp.float32)
    rows = []
    for base in (0, 6):
        first = a[base : base + 1] + a[base + 2 : base + 3] + a[base + 4 : base + 5]
        second = a[base + 1 : base + 2] + a[base + 3 : base + 4] + a[base + 5 : base + 6]
        rows.append(jnp.concatenate([first, second[:, : ROWS - DEPTH]], axis=1))
    return rows


def prep_kernel(first, role_at, unit, roles, q, g, k, v, lse, delta, out, spare):
    step = pl.program_id(0)
    spare[...] = jnp.zeros_like(spare)
    spare[0, :, 0:ROWS] = lse[...]
    spare[1, :, 0:ROWS] = delta[...]
    for i in range(unit):
        cols = slice(i * DEPTH, (i + 1) * DEPTH)
        out[i, 2 * ROWS :, :] = aux_rows(spare, first + step * unit + i)

        def put(one, two):
            out[i, 0:ROWS, :] = one[:, cols]
            out[i, ROWS : 2 * ROWS, :] = two[:, cols]

        pl.when(roles[role_at] == 1)(functools.partial(put, q, g))
        pl.when(roles[role_at] == 0)(functools.partial(put, k, v))


def prep(first, count, role_at, roles, q, g, k, v, lse, delta, unit=UNIT):
    return call(
        functools.partial(prep_kernel, first, role_at, unit),
        "prep",
        grid=(count // unit,),
        in_specs=[SMEM] + [wide(first, unit)] * 4 + [SMALL] * 2,
        out_specs=tall(SENT, 0, unit),
        out_shape=jax.ShapeDtypeStruct((count, SENT, DEPTH), jnp.bfloat16),
        scratch_shapes=[pltpu.VMEM((2, HEADS, 2 * DEPTH), jnp.float32)],
    )(roles, q, g, k, v, lse, delta)


def edges_kernel(first, roles, q, g, k, v, lse, delta, one, two, back1, back2, dq, dk, dv):
    step = pl.program_id(0)

    def run(role_b):
        for i in range(UNIT):
            cols = slice(i * DEPTH, (i + 1) * DEPTH)
            head = first + step * UNIT + i
            own_lse, own_delta = lse[pl.ds(head, 1), :], delta[pl.ds(head, 1), :]

            def joined(own, at):
                rows = slice(at * ROWS, (at + 1) * ROWS)
                return jnp.concatenate([own[:, cols], one[i, rows, :], two[i, rows, :]], axis=0)

            if role_b:
                aux = [read_aux(x[i, 2 * ROWS :, :]) for x in (one, two)]
                all_lse = jnp.concatenate([own_lse, aux[0][0], aux[1][0]], axis=1)
                all_delta = jnp.concatenate([own_delta, aux[0][1], aux[1][1]], axis=1)
                shape = (ROWS, 3 * ROWS)
                keys = lax.broadcasted_iota(jnp.int32, shape, 0)
                mask = keys <= lax.broadcasted_iota(jnp.int32, shape, 1)
                key, value, query = pair(
                    k[:, cols], v[:, cols], joined(q, 0), joined(g, 1), all_lse, all_delta, mask
                )
                dk[:, cols] = key.astype(jnp.bfloat16)
                dv[:, cols] = value.astype(jnp.bfloat16)
                query = query.astype(jnp.bfloat16)
                dq[:, cols] = query[0:ROWS]
                for n, back in ((1, back1), (2, back2)):
                    back[i, 0:ROWS, :] = query[n * ROWS : (n + 1) * ROWS]
                    back[i, ROWS:, :] = jnp.zeros((ROWS, DEPTH), jnp.bfloat16)
            else:
                shape = (3 * ROWS, ROWS)
                keys = lax.broadcasted_iota(jnp.int32, shape, 0)
                mask = keys <= lax.broadcasted_iota(jnp.int32, shape, 1)
                mask = jnp.logical_or(mask, keys >= ROWS)
                key, value, query = pair(
                    joined(k, 0), joined(v, 1), q[:, cols], g[:, cols], own_lse, own_delta, mask
                )
                dq[:, cols] = query.astype(jnp.bfloat16)
                key, value = key.astype(jnp.bfloat16), value.astype(jnp.bfloat16)
                dk[:, cols] = key[0:ROWS]
                dv[:, cols] = value[0:ROWS]
                for n, back in ((1, back1), (2, back2)):
                    back[i, 0:ROWS, :] = key[n * ROWS : (n + 1) * ROWS]
                    back[i, ROWS:, :] = value[n * ROWS : (n + 1) * ROWS]

    pl.when(roles[1] == 1)(functools.partial(run, True))
    pl.when(roles[1] == 0)(functools.partial(run, False))


def edges(first, count, roles, q, g, k, v, lse, delta, one, two):
    own = wide(0)
    return call(
        functools.partial(edges_kernel, first),
        "edges",
        limit=24 * 1024 * 1024,
        grid=(count // UNIT,),
        in_specs=[SMEM] + [wide(first)] * 4 + [SMALL] * 2 + [tall(SENT)] * 2,
        out_specs=[tall(BACK)] * 2 + [own] * 3,
        out_shape=[jax.ShapeDtypeStruct((count, BACK, DEPTH), jnp.bfloat16)] * 2
        + [jax.ShapeDtypeStruct((ROWS, count * DEPTH), jnp.bfloat16)] * 3,
    )(roles, q, g, k, v, lse, delta, one, two)


def add_kernel(a, b, out):
    out[...] = (a[...].astype(jnp.float32) + b[...].astype(jnp.float32)).astype(jnp.bfloat16)


def add(a, b):
    vmem = pl.BlockSpec(memory_space=pltpu.VMEM)
    return call(
        add_kernel,
        "add",
        limit=24 * 1024 * 1024,
        in_specs=[vmem] * 2,
        out_specs=vmem,
        out_shape=jax.ShapeDtypeStruct(a.shape, a.dtype),
    )(a, b)


def carry_kernel(roles, recv, held, back, mine):
    layer = roles[3]
    r1, r2 = recv[0:ROWS], recv[ROWS : 2 * ROWS]
    l1, l2 = held[0, 0:ROWS], held[0, ROWS : 2 * ROWS]

    def put(ref, one, two):
        ref[0:ROWS, :] = one.astype(jnp.bfloat16)
        if two is None:
            ref[ROWS:, :] = jnp.zeros((ROWS, DEPTH), jnp.bfloat16)
        else:
            ref[ROWS:, :] = two.astype(jnp.bfloat16)

    @pl.when(layer <= 4)
    def _():
        lse, delta = read_aux(recv[2 * ROWS :])
        key, value, query = pair(l1, l2, r1, r2, lse, delta)
        put(back, query, None)
        put(mine, key, value)

    @pl.when(layer > 4)
    def _():
        lse, delta = read_aux(held[0, 2 * ROWS :])
        key, value, query = pair(r1, r2, l1, l2, lse, delta)
        put(back, key, value)
        put(mine, query, None)


def carry(roles, recv, spread_in):
    out = pl.BlockSpec((BACK, DEPTH), lambda i: (0, 0))
    return call(
        carry_kernel,
        "carry",
        limit=24 * 1024 * 1024,
        grid=(1,),
        in_specs=[
            SMEM,
            pl.BlockSpec((SENT, DEPTH), lambda i: (0, 0)),
            pl.BlockSpec((1, SENT, DEPTH), lambda i: (LAYER - 1, 0, 0)),
        ],
        out_specs=[out] * 2,
        out_shape=[jax.ShapeDtypeStruct((BACK, DEPTH), jnp.bfloat16)] * 2,
    )(roles, recv, spread_in)


def ends_kernel(home, mine, out):
    out[...] = jnp.zeros_like(out)
    out[0] = home[...]
    out[LAYER - 1] = mine[...]


def ends(home, mine):
    vmem = pl.BlockSpec(memory_space=pltpu.VMEM)
    return call(
        ends_kernel,
        "ends",
        limit=48 * 1024 * 1024,
        in_specs=[vmem] * 2,
        out_specs=vmem,
        out_shape=jax.ShapeDtypeStruct((LAYER, BACK, DEPTH), jnp.bfloat16),
    )(home, mine)


def final_kernel(roles, dq, dk, dv, home, carried, *refs):
    oq, ok, ov = refs[-3:]
    layer, place = roles[3], roles[4]
    home_q = layer >= 2
    carried_q = jnp.where(place == 0, layer >= 3, layer >= 5)
    for i in range(UNIT):
        cols = slice(i * DEPTH, (i + 1) * DEPTH)
        f32 = [x[:, cols].astype(jnp.float32) for x in (dq, dk, dv)]
        h1 = home[i, 0:ROWS, :].astype(jnp.float32)
        h2 = home[i, ROWS:, :].astype(jnp.float32)
        c1 = carried[i, 0:ROWS, :].astype(jnp.float32)
        c2 = carried[i, ROWS:, :].astype(jnp.float32)
        to_q = jnp.where(home_q, h1, 0.0) + jnp.where(carried_q, c1, 0.0)
        to_k = jnp.where(home_q, 0.0, h1) + jnp.where(carried_q, 0.0, c1)
        to_v = jnp.where(home_q, 0.0, h2) + jnp.where(carried_q, 0.0, c2)
        oq[:, cols] = (f32[0] + to_q).astype(jnp.bfloat16)
        ok[:, cols] = (f32[1] + to_k).astype(jnp.bfloat16)
        ov[:, cols] = (f32[2] + to_v).astype(jnp.bfloat16)


def final(first, count, roles, own, home, carried, outs):
    held = list(outs) if outs else []
    return call(
        final_kernel,
        "final",
        limit=24 * 1024 * 1024,
        grid=(count // UNIT,),
        in_specs=[SMEM] + [wide(0)] * 3 + [tall(BACK), tall(BACK, first)] + [ANY] * len(held),
        out_specs=[wide(first)] * 3,
        out_shape=[jax.ShapeDtypeStruct((ROWS, HEADS * DEPTH), jnp.bfloat16)] * 3,
        input_output_aliases={6 + n: n for n in range(len(held))},
    )(roles, *own, home, carried, *held)


def on_device(queries, keys, values, out_grad, log_sum, delta):
    count = lax.axis_size("seq")
    position = lax.axis_index("seq")
    layer, place = position // LAYER, position % LAYER
    groups = [list(range(s, s + LAYER)) for s in range(0, count, LAYER)]
    inputs = (queries, out_grad, keys, values, log_sum, delta)

    def ring(x, by):
        return lax.ppermute(x, "seq", [(i, (i + by) % count) for i in range(count)])

    def beside(x, by):
        pairs = [(i, i + by) for i in range(count) if (i + by) // LAYER == i // LAYER]
        return lax.ppermute(x, "seq", pairs)

    def spread(x):
        return lax.all_to_all(x, "seq", 0, 0, axis_index_groups=groups, tiled=True)

    carry_q = jnp.where(place == LAYER - 1, layer >= 5, layer >= 3)
    roles = jnp.stack([layer >= 2, layer <= 5, carry_q, layer, place]).astype(jnp.int32)
    firsts = [sum(CHUNKS[:n]) for n in range(len(CHUNKS))]
    total = len(CHUNKS)

    sent = [None] * total
    sent[0] = prep(firsts[0], CHUNKS[0], 0, roles, *inputs)
    roles1 = together(roles, sent[0])[0]
    spread_in = spread(prep(0, HEADS, 2, roles1, *inputs, unit=4))
    for c in range(1, total):
        sent[c] = prep(firsts[c], CHUNKS[c], 0, roles1, *inputs)

    recv, near, own, summed, home = ([None] * total for _ in range(5))
    carried = carry_back = packed = None
    recv[0] = arrived(ring(sent[0], -2 * LAYER), *sent[1:])
    carry_recv = arrived(ring(spread_in[0], -3 * LAYER), us=0)
    for c in range(total):
        near[c] = beside(recv[c], -1)
        if c + 1 < total:
            coming = ring(together(sent[c + 1], recv[c])[0], -2 * LAYER)
        waits = [[spread_in], [packed], [home[0]]][min(c, 2)]
        near[c] = together(near[c], *waits, *summed[max(c - 1, 0) : c])[0]
        b1, b2, *own[c] = edges(firsts[c], CHUNKS[c], roles, *inputs, recv[c], near[c])
        from_near = beside(b2, 1)
        if c == 0:
            carry_back, mine = carry(roles, together(carry_recv, b1)[0], spread_in)
            carry_home = arrived(ring(carry_back, 3 * LAYER), us=5)
            b1 = together(b1, carry_back)[0]
        if c + 1 < total:
            recv[c + 1] = arrived(coming, b1)
            from_near = together(from_near, recv[c + 1])[0]
        summed[c] = add(b1, from_near)
        home_sent = summed[c]
        home[c] = ring(summed[c], 2 * LAYER)
        if c == 0:
            home[c] = arrived(home[c])
            packed = ends(together(carry_home, home_sent)[0], mine)
            carried = spread(packed)

    outs = None
    for c in range(total):
        if c:
            home[c] = arrived(home[c], summed[-1], *outs)
        outs = final(firsts[c], CHUNKS[c], roles, own[c], home[c], carried, outs)
    return tuple(outs)


def solution(mesh):
    rows = P(("grp", "seq"), None)
    cols = P(None, ("grp", "seq"))
    return jax.shard_map(
        on_device,
        mesh=mesh,
        in_specs=(rows, rows, rows, rows, cols, cols),
        out_specs=(rows, rows, rows),
        check_vma=False,
    )
```

time: 556 us -> 185 us (0.33)
  the two profiles are of different devices: /device:TPU:22 before, /device:TPU:5 now
where the time goes in v2:
time: 185 us; the launch traced here: 183 us
  starting transfers between devices  64.8 us (35%)
  waiting for transfers between devices  58.7 us (32%)
  Pallas kernels  36.5 us (20%)
  local copies, waits for them, and re-layouts  21.6 us (12%)
    ppermute x8, starting transfers between devices, ring(): return lax.ppermute(x, 'seq', [(i, (i + by) % count) for i in range(count)])  36.4 us
    ppermute x8, waiting for transfers between devices, ring(): return lax.ppermute(x, 'seq', [(i, (i + by) % count) for i in range(count)])  32 us
    ppermute x6, waiting for transfers between devices, beside(): return lax.ppermute(x, 'seq', pairs)  26.8 us
    unnamed x84, local copies, waits for them, and re-layouts  20.1 us
    ppermute x6, starting transfers between devices, beside(): return lax.ppermute(x, 'seq', pairs)  16.4 us
    pallas_call x4, Pallas kernels, prep(): call(functools.partial(prep_kernel, first, role_at, unit), 'prep', grid=(...  12.3 us
    all_to_all x2, starting transfers between devices, spread(): return lax.all_to_all(x, 'seq', 0, 0, axis_index_groups=groups, tiled=True)  12 us
    pallas_call x3, Pallas kernels, edges(): call(functools.partial(edges_kernel, first), 'edges', limit=24 * 1024 * 1...  11.9 us
  transfers between devices with their start and end apart: 16, of which 8 were waited for; matrix products, arithmetic and copies ran while one was open for 0% of the time, Pallas kernels for 17%

profile of v2, /device:TPU:5, one launch (start us, length us, event | category | flops | bytes accessed | tf_op | source)
XLA Modules:
  0.0 182.8 jit_solution(12823393511292507234)
XLA Ops:
  1.3 3.1 %prep.4 = bf16[6,336,128]{2,1,0:T(8,128)(2,1)} custom-call(s32[5]{0:T(128)} %stack.35.roles, bf16[160,2048]{1,0:T(8,128)(2,1)} %q.13, bf16[160,2048]{1,0:T(8,128)(2,1)} %g.13, bf16[160,2048]{1,0:T(8,128)(2,1)} %k.13, bf16[160,2048]{1,0:T(8,128)(2,1)} %v.13, f32[16,160]{1,0:T(8,128)} %lse.13, f32[16,160]{1,0:T(8,128)} %delta.13), custom_call_target="tpu_custom_call" | custom-call | flops 1000 | bytes 1000 | tf_op jit(solution)/shard_map/prep/pallas_call | solution.py:133
  4.3 11.5 %collective-permute-start = (bf16[6,336,128]{2,1,0:T(8,128)(2,1)}, bf16[6,336,128]{2,1,0:T(8,128)(2,1)S(1)}, u32[]{:S(2)}, u32[]{:S(2)}) collective-permute-start(bf16[6,336,128]{2,1,0:T(8,128)(2,1)} %prep.4), channel_id=1, source_target_pairs={{0,384},{4,388},{8,392},{12,396},{16,400},{20,404},{24,408},{28,41... | collective-permute-start | bytes 1548296 | tf_op jit(solution)/shard_map/ppermute | solution.py:328
  15.8 4.1 %prep.7 = bf16[16,336,128]{2,1,0:T(8,128)(2,1)} custom-call(s32[5]{0:T(128)} %stack.35.roles, bf16[160,2048]{1,0:T(8,128)(2,1)} %q.13, bf16[160,2048]{1,0:T(8,128)(2,1)} %g.13, bf16[160,2048]{1,0:T(8,128)(2,1)} %k.13, bf16[160,2048]{1,0:T(8,128)(2,1)} %v.13, f32[16,160]{1,0:T(8,128)} %lse.13, f32[16,160]{1,0:T(8,128)} %delta.13), custom_call_target="tpu_custom_call" | custom-call | flops 1000 | bytes 1000 | tf_op jit(solution)/shard_map/prep/pallas_call | solution.py:133
  20.0 6.9 %all-to-all-start = ((bf16[16,336,128]{2,1,0:T(8,128)(2,1)}), bf16[16,336,128]{2,1,0:T(8,128)(2,1)}, u32[]{:S(2)}, u32[]{:S(2)}) async-start(bf16[16,336,128]{2,1,0:T(8,128)(2,1)} %prep.7), calls=%async_computation | async-start | bytes 2752512 | tf_op jit(solution)/shard_map/all_to_all | solution.py:335
  26.9 3.1 %prep.6 = bf16[6,336,128]{2,1,0:T(8,128)(2,1)} custom-call(s32[5]{0:T(128)} %stack.35.roles, bf16[160,2048]{1,0:T(8,128)(2,1)} %q.13, bf16[160,2048]{1,0:T(8,128)(2,1)} %g.13, bf16[160,2048]{1,0:T(8,128)(2,1)} %k.13, bf16[160,2048]{1,0:T(8,128)(2,1)} %v.13, f32[16,160]{1,0:T(8,128)} %lse.13, f32[16,160]{1,0:T(8,128)} %delta.13), custom_call_target="tpu_custom_call" | custom-call | flops 1000 | bytes 1000 | tf_op jit(solution)/shard_map/prep/pallas_call | solution.py:133
  29.9 2.0 %prep.5 = bf16[4,336,128]{2,1,0:T(8,128)(2,1)} custom-call(s32[5]{0:T(128)} %stack.35.roles, bf16[160,2048]{1,0:T(8,128)(2,1)} %q.13, bf16[160,2048]{1,0:T(8,128)(2,1)} %g.13, bf16[160,2048]{1,0:T(8,128)(2,1)} %k.13, bf16[160,2048]{1,0:T(8,128)(2,1)} %v.13, f32[16,160]{1,0:T(8,128)} %lse.13, f32[16,160]{1,0:T(8,128)} %delta.13), custom_call_target="tpu_custom_call" | custom-call | flops 1000 | bytes 1000 | tf_op jit(solution)/shard_map/prep/pallas_call | solution.py:133
  32.8 4.6 %collective-permute-start.2 = (bf16[6,336,128]{2,1,0:T(8,128)(2,1)}, bf16[6,336,128]{2,1,0:T(8,128)(2,1)}, u32[]{:S(2)}, u32[]{:S(2)}) collective-permute-start(bf16[6,336,128]{2,1,0:T(8,128)(2,1)} %arrived.8.one), channel_id=1, source_target_pairs={{4,0},{8,4},{12,8},{16,12},{20,16},{24,20},{28,24},{32,28},{36,32}... | collective-permute-start | bytes 1548296 | tf_op jit(solution)/shard_map/ppermute | solution.py:332
  37.4 7.8 %collective-permute-start.1 = (bf16[6,336,128]{2,1,0:T(8,128)(2,1)}, bf16[6,336,128]{2,1,0:T(8,128)(2,1)S(1)}, u32[]{:S(2)}, u32[]{:S(2)}) collective-permute-start(bf16[6,336,128]{2,1,0:T(8,128)(2,1)} %prep.6), channel_id=1, source_target_pairs={{0,384},{4,388},{8,392},{12,396},{16,400},{20,404},{24,408},{28,41... | collective-permute-start | bytes 1548296 | tf_op jit(solution)/shard_map/ppermute | solution.py:328
  48.1 7.5 %collective-permute-done.2.two = bf16[6,336,128]{2,1,0:T(8,128)(2,1)} collective-permute-done((bf16[6,336,128]{2,1,0:T(8,128)(2,1)}, bf16[6,336,128]{2,1,0:T(8,128)(2,1)}, u32[]{:S(2)}, u32[]{:S(2)}) %collective-permute-start.2) | collective-permute-done | bytes 516128 | tf_op jit(solution)/shard_map/ppermute | solution.py:332
  56.7 4.6 %edges.3 = (bf16[6,320,128]{2,1,0:T(8,128)(2,1)S(1)}, bf16[6,320,128]{2,1,0:T(8,128)(2,1)}, bf16[160,768]{1,0:T(8,128)(2,1)S(1)}, bf16[160,768]{1,0:T(8,128)(2,1)S(1)}, bf16[160,768]{1,0:T(8,128)(2,1)S(1)}) custom-call(s32[5]{0:T(128)S(1)} %copy-done.41, bf16[160,2048]{1,0:T(8,128)(2,1)S(1)} %copy-done, bf16[160,2048]{1,0:T(8,128)(2,1)S(1)} %copy-done.1, ...), custom_call_target="tpu_custom_call" | custom-call | flops 1000 | bytes 1000 | tf_op jit(solution)/shard_map/edges/pallas_call | solution.py:196
  63.5 2.1 %collective-permute-start.7 = (bf16[6,320,128]{2,1,0:T(8,128)(2,1)}, bf16[6,320,128]{2,1,0:T(8,128)(2,1)}, u32[]{:S(2)}, u32[]{:S(2)}) collective-permute-start(bf16[6,320,128]{2,1,0:T(8,128)(2,1)} %get-tuple-element.52), channel_id=1, source_target_pairs={{0,4},{4,8},{8,12},{12,16},{16,20},{20,24},{24,28},{28,32},{32,36}... | collective-permute-start | bytes 1474568 | tf_op jit(solution)/shard_map/ppermute | solution.py:332
  65.6 12.0 %collective-permute-done.3.x = bf16[336,128]{1,0:T(8,128)(2,1)S(1)} collective-permute-done((bf16[336,128]{1,0:T(8,128)(2,1)S(1)}, bf16[336,128]{1,0:T(8,128)(2,1)S(1)}, u32[]{:S(2)}, u32[]{:S(2)}) %collective-permute-start.3) | collective-permute-done | bytes 86048 | tf_op jit(solution)/shard_map/ppermute | solution.py:328
  79.1 2.0 %carry.1 = (bf16[320,128]{1,0:T(8,128)(2,1)}, bf16[320,128]{1,0:T(8,128)(2,1)S(1)}) custom-call(s32[5]{0:T(128)S(1)} %copy-done.41, bf16[336,128]{1,0:T(8,128)(2,1)S(1)} %copy-done.16, bf16[16,336,128]{2,1,0:T(8,128)(2,1)} %all-to-all-done.held), custom_call_target="tpu_custom_call" | custom-call | flops 1000 | bytes 1000 | tf_op jit(solution)/shard_map/carry/pallas_call | solution.py:253
  84.4 2.2 %collective-permute-start.5 = (bf16[6,336,128]{2,1,0:T(8,128)(2,1)}, bf16[6,336,128]{2,1,0:T(8,128)(2,1)}, u32[]{:S(2)}, u32[]{:S(2)}) collective-permute-start(bf16[6,336,128]{2,1,0:T(8,128)(2,1)} %arrived.10.one), channel_id=1, source_target_pairs={{4,0},{8,4},{12,8},{16,12},{20,16},{24,20},{28,24},{32,28},{36,32}... | collective-permute-start | bytes 1548296 | tf_op jit(solution)/shard_map/ppermute | solution.py:332
  86.7 4.1 %collective-permute-start.4 = (bf16[4,336,128]{2,1,0:T(8,128)(2,1)}, bf16[4,336,128]{2,1,0:T(8,128)(2,1)S(1)}, u32[]{:S(2)}, u32[]{:S(2)}) collective-permute-start(bf16[4,336,128]{2,1,0:T(8,128)(2,1)} %prep.5), channel_id=1, source_target_pairs={{0,384},{4,388},{8,392},{12,396},{16,400},{20,404},{24,408},{28,41... | collective-permute-start | bytes 1032200 | tf_op jit(solution)/shard_map/ppermute | solution.py:328
  90.8 2.0 %collective-permute-done.6.x = bf16[320,128]{1,0:T(8,128)(2,1)S(1)} collective-permute-done((bf16[320,128]{1,0:T(8,128)(2,1)}, bf16[320,128]{1,0:T(8,128)(2,1)S(1)}, u32[]{:S(2)}, u32[]{:S(2)}) %collective-permute-start.6) | collective-permute-done | bytes 81952 | tf_op jit(solution)/shard_map/ppermute | solution.py:328
  93.4 2.0 %add.9 = bf16[6,320,128]{2,1,0:T(8,128)(2,1)} custom-call(bf16[6,320,128]{2,1,0:T(8,128)(2,1)S(1)} %get-tuple-element.49.a, bf16[6,320,128]{2,1,0:T(8,128)(2,1)} %collective-permute-done.7.b), custom_call_target="tpu_custom_call" | custom-call | flops 1000 | bytes 1000 | tf_op jit(solution)/shard_map/add/pallas_call | solution.py:214
  98.6 5.1 %all-to-all-start.1 = ((bf16[16,320,128]{2,1,0:T(8,128)(2,1)}), bf16[16,320,128]{2,1,0:T(8,128)(2,1)}, u32[]{:S(2)}, u32[]{:S(2)}) async-start(bf16[16,320,128]{2,1,0:T(8,128)(2,1)} %copy-done.4), calls=%async_computation.1 | async-start | bytes 2621440 | tf_op jit(solution)/shard_map/all_to_all | solution.py:335
  103.7 4.7 %edges.4 = (bf16[6,320,128]{2,1,0:T(8,128)(2,1)S(1)}, bf16[6,320,128]{2,1,0:T(8,128)(2,1)}, bf16[160,768]{1,0:T(8,128)(2,1)S(1)}, bf16[160,768]{1,0:T(8,128)(2,1)S(1)}, bf16[160,768]{1,0:T(8,128)(2,1)S(1)}) custom-call(s32[5]{0:T(128)S(1)} %copy-done.41, bf16[160,2048]{1,0:T(8,128)(2,1)S(1)} %copy-done, bf16[160,2048]{1,0:T(8,128)(2,1)S(1)} %copy-done.1, ...), custom_call_target="tpu_custom_call" | custom-call | flops 1000 | bytes 1000 | tf_op jit(solution)/shard_map/edges/pallas_call | solution.py:196
  110.5 3.1 %collective-permute-start.10 = (bf16[6,320,128]{2,1,0:T(8,128)(2,1)}, bf16[6,320,128]{2,1,0:T(8,128)(2,1)S(1)}, u32[]{:S(2)}, u32[]{:S(2)}) collective-permute-start(bf16[6,320,128]{2,1,0:T(8,128)(2,1)} %get-tuple-element.59), channel_id=1, source_target_pairs={{0,4},{4,8},{8,12},{12,16},{16,20},{20,24},{24,28},{28,32},{32,36}... | collective-permute-start | bytes 1474568 | tf_op jit(solution)/shard_map/ppermute | solution.py:332
  113.6 5.0 %collective-permute-done.4.x = bf16[4,336,128]{2,1,0:T(8,128)(2,1)S(1)} collective-permute-done((bf16[4,336,128]{2,1,0:T(8,128)(2,1)}, bf16[4,336,128]{2,1,0:T(8,128)(2,1)S(1)}, u32[]{:S(2)}, u32[]{:S(2)}) %collective-permute-start.4) | collective-permute-done | bytes 344096 | tf_op jit(solution)/shard_map/ppermute | solution.py:328
  119.4 2.4 %collective-permute-start.8 = (bf16[4,336,128]{2,1,0:T(8,128)(2,1)}, bf16[4,336,128]{2,1,0:T(8,128)(2,1)S(1)}, u32[]{:S(2)}, u32[]{:S(2)}) collective-permute-start(bf16[4,336,128]{2,1,0:T(8,128)(2,1)} %arrived.12.one), channel_id=1, source_target_pairs={{4,0},{8,4},{12,8},{16,12},{20,16},{24,20},{28,24},{32,28},{36,32}... | collective-permute-start | bytes 1032200 | tf_op jit(solution)/shard_map/ppermute | solution.py:332
  121.7 9.7 %collective-permute-done.10.b = bf16[6,320,128]{2,1,0:T(8,128)(2,1)S(1)} collective-permute-done((bf16[6,320,128]{2,1,0:T(8,128)(2,1)}, bf16[6,320,128]{2,1,0:T(8,128)(2,1)S(1)}, u32[]{:S(2)}, u32[]{:S(2)}) %collective-permute-start.10) | collective-permute-done | bytes 491552 | tf_op jit(solution)/shard_map/ppermute | solution.py:332
  133.4 3.1 %collective-permute-start.13 = (bf16[6,320,128]{2,1,0:T(8,128)(2,1)S(1)}, bf16[6,320,128]{2,1,0:T(8,128)(2,1)}, u32[]{:S(2)}, u32[]{:S(2)}) collective-permute-start(bf16[6,320,128]{2,1,0:T(8,128)(2,1)S(1)} %add.10), channel_id=1, source_target_pairs={{0,128},{4,132},{8,136},{12,140},{16,144},{20,148},{24,152},{28,15... | collective-permute-start | bytes 1474568 | tf_op jit(solution)/shard_map/ppermute | solution.py:328
  136.5 2.6 %edges.5 = (bf16[4,320,128]{2,1,0:T(8,128)(2,1)S(1)}, bf16[4,320,128]{2,1,0:T(8,128)(2,1)S(1)}, bf16[160,512]{1,0:T(8,128)(2,1)S(1)}, bf16[160,512]{1,0:T(8,128)(2,1)S(1)}, bf16[160,512]{1,0:T(8,128)(2,1)S(1)}) custom-call(s32[5]{0:T(128)S(1)} %copy-done.41, bf16[160,2048]{1,0:T(8,128)(2,1)S(1)} %copy-done, bf16[160,2048]{1,0:T(8,128)(2,1)S(1)} %copy-done.1, ...), custom_call_target="tpu_custom_call" | custom-call | flops 1000 | bytes 1000 | tf_op jit(solution)/shard_map/edges/pallas_call | solution.py:196
  139.2 1.9 %collective-permute-start.11 = (bf16[4,320,128]{2,1,0:T(8,128)(2,1)S(1)}, bf16[4,320,128]{2,1,0:T(8,128)(2,1)S(1)}, u32[]{:S(2)}, u32[]{:S(2)}) collective-permute-start(bf16[4,320,128]{2,1,0:T(8,128)(2,1)S(1)} %get-tuple-element.66), channel_id=1, source_target_pairs={{0,4},{4,8},{8,12},{12,16},{16,20},{20,24},{24,28},{28,32},{32,36}... | collective-permute-start | bytes 983048 | tf_op jit(solution)/shard_map/ppermute | solution.py:332
  141.1 9.5 %collective-permute-done.11.b = bf16[4,320,128]{2,1,0:T(8,128)(2,1)S(1)} collective-permute-done((bf16[4,320,128]{2,1,0:T(8,128)(2,1)S(1)}, bf16[4,320,128]{2,1,0:T(8,128)(2,1)S(1)}, u32[]{:S(2)}, u32[]{:S(2)}) %collective-permute-start.11) | collective-permute-done | bytes 327712 | tf_op jit(solution)/shard_map/ppermute | solution.py:332
  150.7 4.2 %collective-permute-start.12 = (bf16[4,320,128]{2,1,0:T(8,128)(2,1)S(1)}, bf16[4,320,128]{2,1,0:T(8,128)(2,1)S(1)}, u32[]{:S(2)}, u32[]{:S(2)}) collective-permute-start(bf16[4,320,128]{2,1,0:T(8,128)(2,1)S(1)} %add.11), channel_id=1, source_target_pairs={{0,128},{4,132},{8,136},{12,140},{16,144},{20,148},{24,152},{28,15... | collective-permute-start | bytes 983048 | tf_op jit(solution)/shard_map/ppermute | solution.py:328
  157.8 3.1 %final.3 = (bf16[160,2048]{1,0:T(8,128)(2,1)}, bf16[160,2048]{1,0:T(8,128)(2,1)}, bf16[160,2048]{1,0:T(8,128)(2,1)}) custom-call(s32[5]{0:T(128)S(1)} %copy-done.41, bf16[160,768]{1,0:T(8,128)(2,1)S(1)} %copy-done.26, bf16[160,768]{1,0:T(8,128)(2,1)S(1)} %copy-done.28, bf16[160,768]{1,0:T(8,128)(2,1)S(1)} %copy-done.30, bf16[6,320,128]{2,1,0:T(8,128)(2,1)} %arrived.13.home, ...), custom_call_target="tpu_custom_call" | custom-call | flops 1000 | bytes 1000 | tf_op jit(solution)/shard_map/final/pallas_call | solution.py:308
  160.8 10.4 %collective-permute-done.13.x = bf16[6,320,128]{2,1,0:T(8,128)(2,1)} collective-permute-done((bf16[6,320,128]{2,1,0:T(8,128)(2,1)S(1)}, bf16[6,320,128]{2,1,0:T(8,128)(2,1)}, u32[]{:S(2)}, u32[]{:S(2)}) %collective-permute-start.13) | collective-permute-done | bytes 491552 | tf_op jit(solution)/shard_map/ppermute | solution.py:328
  172.4 3.1 %final.4 = (bf16[160,2048]{1,0:T(8,128)(2,1)}, bf16[160,2048]{1,0:T(8,128)(2,1)}, bf16[160,2048]{1,0:T(8,128)(2,1)}) custom-call(s32[5]{0:T(128)S(1)} %copy-done.41, bf16[160,768]{1,0:T(8,128)(2,1)S(1)} %copy-done.20, bf16[160,768]{1,0:T(8,128)(2,1)S(1)} %copy-done.22, ...), custom_call_target="tpu_custom_call", output_to_operand_aliasing={{0}: (6, {}), {1}: (7, {}), {2}: (8, {})} | custom-call | flops 1000 | bytes 1000 | tf_op jit(solution)/shard_map/final/pallas_call | solution.py:308
  175.5 2.6 %collective-permute-done.12.x = bf16[4,320,128]{2,1,0:T(8,128)(2,1)S(1)} collective-permute-done((bf16[4,320,128]{2,1,0:T(8,128)(2,1)S(1)}, bf16[4,320,128]{2,1,0:T(8,128)(2,1)S(1)}, u32[]{:S(2)}, u32[]{:S(2)}) %collective-permute-start.12) | collective-permute-done | bytes 327712 | tf_op jit(solution)/shard_map/ppermute | solution.py:328
  (109 shorter events, 29.7 us)
Async XLA Ops:
  4.3 27.6 %collective-permute-start = (bf16[6,336,128]{2,1,0:T(8,128)(2,1)}, bf16[6,336,128]{2,1,0:T(8,128)(2,1)S(1)}, u32[]{:S(2)}, u32[]{:S(2)}) collective-permute-start(bf16[6,336,128]{2,1,0:T(8,128)(2,1)} %prep.4), channel_id=1, source_target_pairs={{0,384},{4,388},{8,392},{12,396},{16,400},{20,404},{24,408},{28,41... | collective-permute-start | bytes 1548296 | tf_op jit(solution)/shard_map/ppermute | solution.py:328
  20.0 25.3 %all-to-all-start = ((bf16[16,336,128]{2,1,0:T(8,128)(2,1)}), bf16[16,336,128]{2,1,0:T(8,128)(2,1)}, u32[]{:S(2)}, u32[]{:S(2)}) async-start(bf16[16,336,128]{2,1,0:T(8,128)(2,1)} %prep.7), calls=%async_computation | async-start | bytes 2752512 | tf_op jit(solution)/shard_map/all_to_all | solution.py:335
  31.9 23.7 %copy-start = (bf16[160,2048]{1,0:T(8,128)(2,1)S(1)}, bf16[160,2048]{1,0:T(8,128)(2,1)}, u32[]{:S(2)}) copy-start(bf16[160,2048]{1,0:T(8,128)(2,1)} %q.13) | copy-start | bytes 1966084
  31.9 23.7 %copy-start.1 = (bf16[160,2048]{1,0:T(8,128)(2,1)S(1)}, bf16[160,2048]{1,0:T(8,128)(2,1)}, u32[]{:S(2)}) copy-start(bf16[160,2048]{1,0:T(8,128)(2,1)} %g.13) | copy-start | bytes 1966084
  31.9 23.7 %copy-start.2 = (bf16[160,2048]{1,0:T(8,128)(2,1)S(1)}, bf16[160,2048]{1,0:T(8,128)(2,1)}, u32[]{:S(2)}) copy-start(bf16[160,2048]{1,0:T(8,128)(2,1)} %k.13) | copy-start | bytes 1966084
  31.9 23.7 %copy-start.3 = (bf16[160,2048]{1,0:T(8,128)(2,1)S(1)}, bf16[160,2048]{1,0:T(8,128)(2,1)}, u32[]{:S(2)}) copy-start(bf16[160,2048]{1,0:T(8,128)(2,1)} %v.13) | copy-start | bytes 1966084
  32.0 23.7 %copy-start.5 = (f32[16,160]{1,0:T(8,128)S(1)}, f32[16,160]{1,0:T(8,128)}, u32[]{:S(2)}) copy-start(f32[16,160]{1,0:T(8,128)} %lse.13) | copy-start | bytes 30724
  32.0 23.7 %copy-start.6 = (f32[16,160]{1,0:T(8,128)S(1)}, f32[16,160]{1,0:T(8,128)}, u32[]{:S(2)}) copy-start(f32[16,160]{1,0:T(8,128)} %delta.13) | copy-start | bytes 30724
  32.0 23.7 %copy-start.41 = (s32[5]{0:T(128)S(1)}, s32[5]{0:T(128)}, u32[]{:S(2)}) copy-start(s32[5]{0:T(128)} %stack.35.roles) | copy-start | bytes 64
  32.8 22.8 %collective-permute-start.2 = (bf16[6,336,128]{2,1,0:T(8,128)(2,1)}, bf16[6,336,128]{2,1,0:T(8,128)(2,1)}, u32[]{:S(2)}, u32[]{:S(2)}) collective-permute-start(bf16[6,336,128]{2,1,0:T(8,128)(2,1)} %arrived.8.one), channel_id=1, source_target_pairs={{4,0},{8,4},{12,8},{16,12},{20,16},{24,20},{28,24},{32,28},{36,32}... | collective-permute-start | bytes 1548296 | tf_op jit(solution)/shard_map/ppermute | solution.py:332
  37.4 46.2 %collective-permute-start.1 = (bf16[6,336,128]{2,1,0:T(8,128)(2,1)}, bf16[6,336,128]{2,1,0:T(8,128)(2,1)S(1)}, u32[]{:S(2)}, u32[]{:S(2)}) collective-permute-start(bf16[6,336,128]{2,1,0:T(8,128)(2,1)} %prep.6), channel_id=1, source_target_pairs={{0,384},{4,388},{8,392},{12,396},{16,400},{20,404},{24,408},{28,41... | collective-permute-start | bytes 1548296 | tf_op jit(solution)/shard_map/ppermute | solution.py:328
  46.2 31.4 %collective-permute-start.3 = (bf16[336,128]{1,0:T(8,128)(2,1)S(1)}, bf16[336,128]{1,0:T(8,128)(2,1)S(1)}, u32[]{:S(2)}, u32[]{:S(2)}) collective-permute-start(bf16[336,128]{1,0:T(8,128)(2,1)S(1)} %slice_bitcast_fusion), channel_id=1, source_target_pairs={{0,320},{4,324},{8,328},{12,332},{16,336},{20,340},{24,344},{28,34... | collective-permute-start | bytes 258056 | tf_op jit(solution)/shard_map/ppermute | solution.py:328
  63.5 30.0 %collective-permute-start.7 = (bf16[6,320,128]{2,1,0:T(8,128)(2,1)}, bf16[6,320,128]{2,1,0:T(8,128)(2,1)}, u32[]{:S(2)}, u32[]{:S(2)}) collective-permute-start(bf16[6,320,128]{2,1,0:T(8,128)(2,1)} %get-tuple-element.52), channel_id=1, source_target_pairs={{0,4},{4,8},{8,12},{12,16},{16,20},{20,24},{24,28},{28,32},{32,36}... | collective-permute-start | bytes 1474568 | tf_op jit(solution)/shard_map/ppermute | solution.py:332
  81.7 11.1 %collective-permute-start.6 = (bf16[320,128]{1,0:T(8,128)(2,1)}, bf16[320,128]{1,0:T(8,128)(2,1)S(1)}, u32[]{:S(2)}, u32[]{:S(2)}) collective-permute-start(bf16[320,128]{1,0:T(8,128)(2,1)} %get-tuple-element.48), channel_id=1, source_target_pairs={{0,192},{4,196},{8,200},{12,204},{16,208},{20,212},{24,216},{28,22... | collective-permute-start | bytes 245768 | tf_op jit(solution)/shard_map/ppermute | solution.py:328
  84.4 19.3 %collective-permute-start.5 = (bf16[6,336,128]{2,1,0:T(8,128)(2,1)}, bf16[6,336,128]{2,1,0:T(8,128)(2,1)}, u32[]{:S(2)}, u32[]{:S(2)}) collective-permute-start(bf16[6,336,128]{2,1,0:T(8,128)(2,1)} %arrived.10.one), channel_id=1, source_target_pairs={{4,0},{8,4},{12,8},{16,12},{20,16},{24,20},{28,24},{32,28},{36,32}... | collective-permute-start | bytes 1548296 | tf_op jit(solution)/shard_map/ppermute | solution.py:332
  86.7 32.0 %collective-permute-start.4 = (bf16[4,336,128]{2,1,0:T(8,128)(2,1)}, bf16[4,336,128]{2,1,0:T(8,128)(2,1)S(1)}, u32[]{:S(2)}, u32[]{:S(2)}) collective-permute-start(bf16[4,336,128]{2,1,0:T(8,128)(2,1)} %prep.5), channel_id=1, source_target_pairs={{0,384},{4,388},{8,392},{12,396},{16,400},{20,404},{24,408},{28,41... | collective-permute-start | bytes 1032200 | tf_op jit(solution)/shard_map/ppermute | solution.py:328
  93.4 3.9 %copy-start.38 = (bf16[320,128]{1,0:T(8,128)(2,1)S(1)}, bf16[320,128]{1,0:T(8,128)(2,1)}, u32[]{:S(2)}) copy-start(bf16[320,128]{1,0:T(8,128)(2,1)} %copy-done.37) | copy-start | bytes 245764
  93.4 3.9 %copy-start.40 = (bf16[320,128]{1,0:T(8,128)(2,1)S(1)}, bf16[320,128]{1,0:T(8,128)(2,1)}, u32[]{:S(2)}) copy-start(bf16[320,128]{1,0:T(8,128)(2,1)} %arrived.11.home) | copy-start | bytes 245764
  95.4 41.1 %collective-permute-start.9 = (bf16[6,320,128]{2,1,0:T(8,128)(2,1)}, bf16[6,320,128]{2,1,0:T(8,128)(2,1)}, u32[]{:S(2)}, u32[]{:S(2)}) collective-permute-start(bf16[6,320,128]{2,1,0:T(8,128)(2,1)} %add.9), channel_id=1, source_target_pairs={{0,128},{4,132},{8,136},{12,140},{16,144},{20,148},{24,152},{28,15... | collective-permute-start | bytes 1474568 | tf_op jit(solution)/shard_map/ppermute | solution.py:328
  97.5 1.1 copy-start.4
  98.6 5.1 %copy-start.8 = (bf16[6,336,128]{2,1,0:T(8,128)(2,1)S(1)}, bf16[6,336,128]{2,1,0:T(8,128)(2,1)}, u32[]{:S(2)}) copy-start(bf16[6,336,128]{2,1,0:T(8,128)(2,1)} %arrived.10.one) | copy-start | bytes 1548292
  98.6 56.3 %all-to-all-start.1 = ((bf16[16,320,128]{2,1,0:T(8,128)(2,1)}), bf16[16,320,128]{2,1,0:T(8,128)(2,1)}, u32[]{:S(2)}, u32[]{:S(2)}) async-start(bf16[16,320,128]{2,1,0:T(8,128)(2,1)} %copy-done.4), calls=%async_computation.1 | async-start | bytes 2621440 | tf_op jit(solution)/shard_map/all_to_all | solution.py:335
  110.5 20.9 %collective-permute-start.10 = (bf16[6,320,128]{2,1,0:T(8,128)(2,1)}, bf16[6,320,128]{2,1,0:T(8,128)(2,1)S(1)}, u32[]{:S(2)}, u32[]{:S(2)}) collective-permute-start(bf16[6,320,128]{2,1,0:T(8,128)(2,1)} %get-tuple-element.59), channel_id=1, source_target_pairs={{0,4},{4,8},{8,12},{12,16},{16,20},{20,24},{24,28},{28,32},{32,36}... | collective-permute-start | bytes 1474568 | tf_op jit(solution)/shard_map/ppermute | solution.py:332
  119.4 17.2 %collective-permute-start.8 = (bf16[4,336,128]{2,1,0:T(8,128)(2,1)}, bf16[4,336,128]{2,1,0:T(8,128)(2,1)S(1)}, u32[]{:S(2)}, u32[]{:S(2)}) collective-permute-start(bf16[4,336,128]{2,1,0:T(8,128)(2,1)} %arrived.12.one), channel_id=1, source_target_pairs={{4,0},{8,4},{12,8},{16,12},{20,16},{24,20},{28,24},{32,28},{36,32}... | collective-permute-start | bytes 1032200 | tf_op jit(solution)/shard_map/ppermute | solution.py:332
  133.4 3.1 %copy-start.14 = (bf16[4,336,128]{2,1,0:T(8,128)(2,1)S(1)}, bf16[4,336,128]{2,1,0:T(8,128)(2,1)}, u32[]{:S(2)}) copy-start(bf16[4,336,128]{2,1,0:T(8,128)(2,1)} %arrived.12.one) | copy-start | bytes 1032196
  133.4 37.8 %collective-permute-start.13 = (bf16[6,320,128]{2,1,0:T(8,128)(2,1)S(1)}, bf16[6,320,128]{2,1,0:T(8,128)(2,1)}, u32[]{:S(2)}, u32[]{:S(2)}) collective-permute-start(bf16[6,320,128]{2,1,0:T(8,128)(2,1)S(1)} %add.10), channel_id=1, source_target_pairs={{0,128},{4,132},{8,136},{12,140},{16,144},{20,148},{24,152},{28,15... | collective-permute-start | bytes 1474568 | tf_op jit(solution)/shard_map/ppermute | solution.py:328
  139.2 11.5 %copy-start.31 = (bf16[160,512]{1,0:T(8,128)(2,1)}, bf16[160,512]{1,0:T(8,128)(2,1)S(1)}, u32[]{:S(2)}) copy-start(bf16[160,512]{1,0:T(8,128)(2,1)S(1)} %get-tuple-element.62.dq) | copy-start | bytes 491524
  139.2 11.5 %copy-start.33 = (bf16[160,512]{1,0:T(8,128)(2,1)}, bf16[160,512]{1,0:T(8,128)(2,1)S(1)}, u32[]{:S(2)}) copy-start(bf16[160,512]{1,0:T(8,128)(2,1)S(1)} %get-tuple-element.63.dk) | copy-start | bytes 491524
  139.2 11.5 %copy-start.35 = (bf16[160,512]{1,0:T(8,128)(2,1)}, bf16[160,512]{1,0:T(8,128)(2,1)S(1)}, u32[]{:S(2)}) copy-start(bf16[160,512]{1,0:T(8,128)(2,1)S(1)} %get-tuple-element.64.dv) | copy-start | bytes 491524
  139.2 11.4 %collective-permute-start.11 = (bf16[4,320,128]{2,1,0:T(8,128)(2,1)S(1)}, bf16[4,320,128]{2,1,0:T(8,128)(2,1)S(1)}, u32[]{:S(2)}, u32[]{:S(2)}) collective-permute-start(bf16[4,320,128]{2,1,0:T(8,128)(2,1)S(1)} %get-tuple-element.66), channel_id=1, source_target_pairs={{0,4},{4,8},{8,12},{12,16},{16,20},{20,24},{24,28},{28,32},{32,36}... | collective-permute-start | bytes 983048 | tf_op jit(solution)/shard_map/ppermute | solution.py:332
  150.7 27.4 %collective-permute-start.12 = (bf16[4,320,128]{2,1,0:T(8,128)(2,1)S(1)}, bf16[4,320,128]{2,1,0:T(8,128)(2,1)S(1)}, u32[]{:S(2)}, u32[]{:S(2)}) collective-permute-start(bf16[4,320,128]{2,1,0:T(8,128)(2,1)S(1)} %add.11), channel_id=1, source_target_pairs={{0,128},{4,132},{8,136},{12,140},{16,144},{20,148},{24,152},{28,15... | collective-permute-start | bytes 983048 | tf_op jit(solution)/shard_map/ppermute | solution.py:328
  171.2 1.2 copy-start.24
  (26 other events, 21.7 us)

commit v3 on v2

--- a/solution.py
+++ b/solution.py
@@ -72,6 +72,7 @@
         arrived_kernel,
         "arrived",
         us=us,
+        limit=16 * 1024 * 1024,
         in_specs=[ANY],
         out_specs=ANY,
         out_shape=jax.ShapeDtypeStruct(x.shape, x.dtype),

time: 185 us -> 176 us (0.951)
  local copies, waits for them, and re-layouts: 21.6 us -> 9.14 us
  waiting for transfers between devices: 58.7 us -> 65.9 us
  Pallas kernels: 36.5 us -> 33.7 us
    unnamed x84 -> x52, local copies, waits for them, and re-layouts: 20.1 us -> 7.62 us
    ppermute x8, waiting for transfers between devices: 32 us -> 39.7 us  [ring(): return lax.ppermute(x, 'seq', [(i, (i + by) % count) for i in range(count)])]
  transfers between devices with their start and end apart: 16 -> 16, of which waited for: 8 -> 9; matrix products, arithmetic and copies ran while one was open for 0% -> 1% of each run, Pallas kernels for 17% -> 16%
where the time goes in v3:
time: 176 us; the launch traced here: 174 us
  waiting for transfers between devices  65.9 us (37%)
  starting transfers between devices  64.4 us (37%)
  Pallas kernels  33.7 us (19%)
  local copies, waits for them, and re-layouts  9.14 us (5%)
    ppermute x8, waiting for transfers between devices, ring(): return lax.ppermute(x, 'seq', [(i, (i + by) % count) for i in range(count)])  39.7 us
    ppermute x8, starting transfers between devices, ring(): return lax.ppermute(x, 'seq', [(i, (i + by) % count) for i in range(count)])  35.6 us
    ppermute x6, waiting for transfers between devices, beside(): return lax.ppermute(x, 'seq', pairs)  26.2 us
    ppermute x6, starting transfers between devices, beside(): return lax.ppermute(x, 'seq', pairs)  16.9 us
    pallas_call x4, Pallas kernels, prep(): call(functools.partial(prep_kernel, first, role_at, unit), 'prep', grid=(...  12.2 us
    all_to_all x2, starting transfers between devices, spread(): return lax.all_to_all(x, 'seq', 0, 0, axis_index_groups=groups, tiled=True)  12 us
    pallas_call x3, Pallas kernels, edges(): call(functools.partial(edges_kernel, first), 'edges', limit=24 * 1024 * 1...  10.7 us
    pallas_call x3, Pallas kernels, final(): call(final_kernel, 'final', limit=24 * 1024 * 1024, grid=(count // UNIT,)...  8.09 us
  transfers between devices with their start and end apart: 16, of which 9 were waited for; matrix products, arithmetic and copies ran while one was open for 1% of the time, Pallas kernels for 16%

profile of v3, /device:TPU:5, one launch (start us, length us, event | category | flops | bytes accessed | tf_op | source)
XLA Modules:
  0.0 174.2 jit_solution(1859289893571861532)
XLA Ops:
  1.3 3.1 %prep.4 = bf16[6,336,128]{2,1,0:T(8,128)(2,1)} custom-call(s32[5]{0:T(128)} %stack.35.roles, bf16[160,2048]{1,0:T(8,128)(2,1)} %q.13, bf16[160,2048]{1,0:T(8,128)(2,1)} %g.13, bf16[160,2048]{1,0:T(8,128)(2,1)} %k.13, bf16[160,2048]{1,0:T(8,128)(2,1)} %v.13, f32[16,160]{1,0:T(8,128)} %lse.13, f32[16,160]{1,0:T(8,128)} %delta.13), custom_call_target="tpu_custom_call" | custom-call | flops 1000 | bytes 1000 | tf_op jit(solution)/shard_map/prep/pallas_call | solution.py:134
  4.3 11.5 %collective-permute-start = (bf16[6,336,128]{2,1,0:T(8,128)(2,1)}, bf16[6,336,128]{2,1,0:T(8,128)(2,1)}, u32[]{:S(2)}, u32[]{:S(2)}) collective-permute-start(bf16[6,336,128]{2,1,0:T(8,128)(2,1)} %prep.4), channel_id=1, source_target_pairs={{0,384},{4,388},{8,392},{12,396},{16,400},{20,404},{24,408},{28,41... | collective-permute-start | bytes 1548296 | tf_op jit(solution)/shard_map/ppermute | solution.py:329
  15.8 4.1 %prep.7 = bf16[16,336,128]{2,1,0:T(8,128)(2,1)} custom-call(s32[5]{0:T(128)} %stack.35.roles, bf16[160,2048]{1,0:T(8,128)(2,1)} %q.13, bf16[160,2048]{1,0:T(8,128)(2,1)} %g.13, bf16[160,2048]{1,0:T(8,128)(2,1)} %k.13, bf16[160,2048]{1,0:T(8,128)(2,1)} %v.13, f32[16,160]{1,0:T(8,128)} %lse.13, f32[16,160]{1,0:T(8,128)} %delta.13), custom_call_target="tpu_custom_call" | custom-call | flops 1000 | bytes 1000 | tf_op jit(solution)/shard_map/prep/pallas_call | solution.py:134
  20.0 6.9 %all-to-all-start = ((bf16[16,336,128]{2,1,0:T(8,128)(2,1)}), bf16[16,336,128]{2,1,0:T(8,128)(2,1)}, u32[]{:S(2)}, u32[]{:S(2)}) async-start(bf16[16,336,128]{2,1,0:T(8,128)(2,1)} %prep.7), calls=%async_computation | async-start | bytes 2752512 | tf_op jit(solution)/shard_map/all_to_all | solution.py:336
  26.9 3.1 %prep.6 = bf16[6,336,128]{2,1,0:T(8,128)(2,1)} custom-call(s32[5]{0:T(128)} %stack.35.roles, bf16[160,2048]{1,0:T(8,128)(2,1)} %q.13, bf16[160,2048]{1,0:T(8,128)(2,1)} %g.13, bf16[160,2048]{1,0:T(8,128)(2,1)} %k.13, bf16[160,2048]{1,0:T(8,128)(2,1)} %v.13, f32[16,160]{1,0:T(8,128)} %lse.13, f32[16,160]{1,0:T(8,128)} %delta.13), custom_call_target="tpu_custom_call" | custom-call | flops 1000 | bytes 1000 | tf_op jit(solution)/shard_map/prep/pallas_call | solution.py:134
  29.9 2.0 %prep.5 = bf16[4,336,128]{2,1,0:T(8,128)(2,1)} custom-call(s32[5]{0:T(128)} %stack.35.roles, bf16[160,2048]{1,0:T(8,128)(2,1)} %q.13, bf16[160,2048]{1,0:T(8,128)(2,1)} %g.13, bf16[160,2048]{1,0:T(8,128)(2,1)} %k.13, bf16[160,2048]{1,0:T(8,128)(2,1)} %v.13, f32[16,160]{1,0:T(8,128)} %lse.13, f32[16,160]{1,0:T(8,128)} %delta.13), custom_call_target="tpu_custom_call" | custom-call | flops 1000 | bytes 1000 | tf_op jit(solution)/shard_map/prep/pallas_call | solution.py:134
  32.0 4.7 %collective-permute-start.2 = (bf16[6,336,128]{2,1,0:T(8,128)(2,1)}, bf16[6,336,128]{2,1,0:T(8,128)(2,1)}, u32[]{:S(2)}, u32[]{:S(2)}) collective-permute-start(bf16[6,336,128]{2,1,0:T(8,128)(2,1)} %arrived.8.one), channel_id=1, source_target_pairs={{4,0},{8,4},{12,8},{16,12},{20,16},{24,20},{28,24},{32,28},{36,32}... | collective-permute-start | bytes 1548296 | tf_op jit(solution)/shard_map/ppermute | solution.py:333
  36.8 7.7 %collective-permute-start.1 = (bf16[6,336,128]{2,1,0:T(8,128)(2,1)}, bf16[6,336,128]{2,1,0:T(8,128)(2,1)S(1)}, u32[]{:S(2)}, u32[]{:S(2)}) collective-permute-start(bf16[6,336,128]{2,1,0:T(8,128)(2,1)} %prep.6), channel_id=1, source_target_pairs={{0,384},{4,388},{8,392},{12,396},{16,400},{20,404},{24,408},{28,41... | collective-permute-start | bytes 1548296 | tf_op jit(solution)/shard_map/ppermute | solution.py:329
  47.3 8.2 %collective-permute-done.2.two = bf16[6,336,128]{2,1,0:T(8,128)(2,1)} collective-permute-done((bf16[6,336,128]{2,1,0:T(8,128)(2,1)}, bf16[6,336,128]{2,1,0:T(8,128)(2,1)}, u32[]{:S(2)}, u32[]{:S(2)}) %collective-permute-start.2) | collective-permute-done | bytes 516128 | tf_op jit(solution)/shard_map/ppermute | solution.py:333
  55.6 4.1 %edges.3 = (bf16[6,320,128]{2,1,0:T(8,128)(2,1)S(1)}, bf16[6,320,128]{2,1,0:T(8,128)(2,1)S(1)}, bf16[160,768]{1,0:T(8,128)(2,1)S(1)}, bf16[160,768]{1,0:T(8,128)(2,1)S(1)}, bf16[160,768]{1,0:T(8,128)(2,1)S(1)}) custom-call(s32[5]{0:T(128)S(1)} %copy-done.25, bf16[160,2048]{1,0:T(8,128)(2,1)S(1)} %copy-done, bf16[160,2048]{1,0:T(8,128)(2,1)S(1)} %copy-done.1, ...), custom_call_target="tpu_custom_call" | custom-call | flops 1000 | bytes 1000 | tf_op jit(solution)/shard_map/edges/pallas_call | solution.py:197
  60.4 2.2 %collective-permute-start.7 = (bf16[6,320,128]{2,1,0:T(8,128)(2,1)S(1)}, bf16[6,320,128]{2,1,0:T(8,128)(2,1)S(1)}, u32[]{:S(2)}, u32[]{:S(2)}) collective-permute-start(bf16[6,320,128]{2,1,0:T(8,128)(2,1)S(1)} %get-tuple-element.52), channel_id=1, source_target_pairs={{0,4},{4,8},{8,12},{12,16},{16,20},{20,24},{24,28},{28,32},{32,36}... | collective-permute-start | bytes 1474568 | tf_op jit(solution)/shard_map/ppermute | solution.py:333
  62.6 14.1 %collective-permute-done.3.x = bf16[336,128]{1,0:T(8,128)(2,1)S(1)} collective-permute-done((bf16[336,128]{1,0:T(8,128)(2,1)S(1)}, bf16[336,128]{1,0:T(8,128)(2,1)S(1)}, u32[]{:S(2)}, u32[]{:S(2)}) %collective-permute-start.3) | collective-permute-done | bytes 86048 | tf_op jit(solution)/shard_map/ppermute | solution.py:329
  78.0 1.9 %collective-permute-start.6 = (bf16[320,128]{1,0:T(8,128)(2,1)S(1)}, bf16[320,128]{1,0:T(8,128)(2,1)S(1)}, u32[]{:S(2)}, u32[]{:S(2)}) collective-permute-start(bf16[320,128]{1,0:T(8,128)(2,1)S(1)} %get-tuple-element.48), channel_id=1, source_target_pairs={{0,192},{4,196},{8,200},{12,204},{16,208},{20,212},{24,216},{28,22... | collective-permute-start | bytes 245768 | tf_op jit(solution)/shard_map/ppermute | solution.py:329
  80.0 2.4 %collective-permute-start.5 = (bf16[6,336,128]{2,1,0:T(8,128)(2,1)S(1)}, bf16[6,336,128]{2,1,0:T(8,128)(2,1)}, u32[]{:S(2)}, u32[]{:S(2)}) collective-permute-start(bf16[6,336,128]{2,1,0:T(8,128)(2,1)S(1)} %arrived.10.one), channel_id=1, source_target_pairs={{4,0},{8,4},{12,8},{16,12},{20,16},{24,20},{28,24},{32,28},{36,32}... | collective-permute-start | bytes 1548296 | tf_op jit(solution)/shard_map/ppermute | solution.py:333
  82.4 4.1 %collective-permute-start.4 = (bf16[4,336,128]{2,1,0:T(8,128)(2,1)}, bf16[4,336,128]{2,1,0:T(8,128)(2,1)S(1)}, u32[]{:S(2)}, u32[]{:S(2)}) collective-permute-start(bf16[4,336,128]{2,1,0:T(8,128)(2,1)} %prep.5), channel_id=1, source_target_pairs={{0,384},{4,388},{8,392},{12,396},{16,400},{20,404},{24,408},{28,41... | collective-permute-start | bytes 1032200 | tf_op jit(solution)/shard_map/ppermute | solution.py:329
  86.5 2.5 %collective-permute-done.6.x = bf16[320,128]{1,0:T(8,128)(2,1)S(1)} collective-permute-done((bf16[320,128]{1,0:T(8,128)(2,1)S(1)}, bf16[320,128]{1,0:T(8,128)(2,1)S(1)}, u32[]{:S(2)}, u32[]{:S(2)}) %collective-permute-start.6) | collective-permute-done | bytes 81952 | tf_op jit(solution)/shard_map/ppermute | solution.py:329
  89.9 1.9 %collective-permute-start.9 = (bf16[6,320,128]{2,1,0:T(8,128)(2,1)}, bf16[6,320,128]{2,1,0:T(8,128)(2,1)}, u32[]{:S(2)}, u32[]{:S(2)}) collective-permute-start(bf16[6,320,128]{2,1,0:T(8,128)(2,1)} %add.9), channel_id=1, source_target_pairs={{0,128},{4,132},{8,136},{12,140},{16,144},{20,148},{24,152},{28,15... | collective-permute-start | bytes 1474568 | tf_op jit(solution)/shard_map/ppermute | solution.py:329
  93.1 5.1 %all-to-all-start.1 = ((bf16[16,320,128]{2,1,0:T(8,128)(2,1)}), bf16[16,320,128]{2,1,0:T(8,128)(2,1)}, u32[]{:S(2)}, u32[]{:S(2)}) async-start(bf16[16,320,128]{2,1,0:T(8,128)(2,1)} %copy-done.4), calls=%async_computation.1 | async-start | bytes 2621440 | tf_op jit(solution)/shard_map/all_to_all | solution.py:336
  98.2 4.0 %edges.4 = (bf16[6,320,128]{2,1,0:T(8,128)(2,1)S(1)}, bf16[6,320,128]{2,1,0:T(8,128)(2,1)S(1)}, bf16[160,768]{1,0:T(8,128)(2,1)S(1)}, bf16[160,768]{1,0:T(8,128)(2,1)S(1)}, bf16[160,768]{1,0:T(8,128)(2,1)S(1)}) custom-call(s32[5]{0:T(128)S(1)} %copy-done.25, bf16[160,2048]{1,0:T(8,128)(2,1)S(1)} %copy-done, bf16[160,2048]{1,0:T(8,128)(2,1)S(1)} %copy-done.1, ...), custom_call_target="tpu_custom_call" | custom-call | flops 1000 | bytes 1000 | tf_op jit(solution)/shard_map/edges/pallas_call | solution.py:197
  102.9 3.1 %collective-permute-start.10 = (bf16[6,320,128]{2,1,0:T(8,128)(2,1)S(1)}, bf16[6,320,128]{2,1,0:T(8,128)(2,1)S(1)}, u32[]{:S(2)}, u32[]{:S(2)}) collective-permute-start(bf16[6,320,128]{2,1,0:T(8,128)(2,1)S(1)} %get-tuple-element.59), channel_id=1, source_target_pairs={{0,4},{4,8},{8,12},{12,16},{16,20},{20,24},{24,28},{28,32},{32,36}... | collective-permute-start | bytes 1474568 | tf_op jit(solution)/shard_map/ppermute | solution.py:333
  106.0 8.9 %collective-permute-done.4.x = bf16[4,336,128]{2,1,0:T(8,128)(2,1)S(1)} collective-permute-done((bf16[4,336,128]{2,1,0:T(8,128)(2,1)}, bf16[4,336,128]{2,1,0:T(8,128)(2,1)S(1)}, u32[]{:S(2)}, u32[]{:S(2)}) %collective-permute-start.4) | collective-permute-done | bytes 344096 | tf_op jit(solution)/shard_map/ppermute | solution.py:329
  114.9 2.3 %collective-permute-start.8 = (bf16[4,336,128]{2,1,0:T(8,128)(2,1)S(1)}, bf16[4,336,128]{2,1,0:T(8,128)(2,1)S(1)}, u32[]{:S(2)}, u32[]{:S(2)}) collective-permute-start(bf16[4,336,128]{2,1,0:T(8,128)(2,1)S(1)} %arrived.12.one), channel_id=1, source_target_pairs={{4,0},{8,4},{12,8},{16,12},{20,16},{24,20},{28,24},{32,28},{36,32}... | collective-permute-start | bytes 1032200 | tf_op jit(solution)/shard_map/ppermute | solution.py:333
  117.2 8.7 %collective-permute-done.10.b = bf16[6,320,128]{2,1,0:T(8,128)(2,1)S(1)} collective-permute-done((bf16[6,320,128]{2,1,0:T(8,128)(2,1)S(1)}, bf16[6,320,128]{2,1,0:T(8,128)(2,1)S(1)}, u32[]{:S(2)}, u32[]{:S(2)}) %collective-permute-start.10) | collective-permute-done | bytes 491552 | tf_op jit(solution)/shard_map/ppermute | solution.py:333
  126.0 2.4 %collective-permute-start.13 = (bf16[6,320,128]{2,1,0:T(8,128)(2,1)S(1)}, bf16[6,320,128]{2,1,0:T(8,128)(2,1)}, u32[]{:S(2)}, u32[]{:S(2)}) collective-permute-start(bf16[6,320,128]{2,1,0:T(8,128)(2,1)S(1)} %add.10), channel_id=1, source_target_pairs={{0,128},{4,132},{8,136},{12,140},{16,144},{20,148},{24,152},{28,15... | collective-permute-start | bytes 1474568 | tf_op jit(solution)/shard_map/ppermute | solution.py:329
  128.4 2.6 %edges.5 = (bf16[4,320,128]{2,1,0:T(8,128)(2,1)S(1)}, bf16[4,320,128]{2,1,0:T(8,128)(2,1)S(1)}, bf16[160,512]{1,0:T(8,128)(2,1)S(1)}, bf16[160,512]{1,0:T(8,128)(2,1)S(1)}, bf16[160,512]{1,0:T(8,128)(2,1)S(1)}) custom-call(s32[5]{0:T(128)S(1)} %copy-done.25, bf16[160,2048]{1,0:T(8,128)(2,1)S(1)} %copy-done, bf16[160,2048]{1,0:T(8,128)(2,1)S(1)} %copy-done.1, ...), custom_call_target="tpu_custom_call" | custom-call | flops 1000 | bytes 1000 | tf_op jit(solution)/shard_map/edges/pallas_call | solution.py:197
  131.1 2.1 %collective-permute-start.11 = (bf16[4,320,128]{2,1,0:T(8,128)(2,1)S(1)}, bf16[4,320,128]{2,1,0:T(8,128)(2,1)S(1)}, u32[]{:S(2)}, u32[]{:S(2)}) collective-permute-start(bf16[4,320,128]{2,1,0:T(8,128)(2,1)S(1)} %get-tuple-element.66), channel_id=1, source_target_pairs={{0,4},{4,8},{8,12},{12,16},{16,20},{20,24},{24,28},{28,32},{32,36}... | collective-permute-start | bytes 983048 | tf_op jit(solution)/shard_map/ppermute | solution.py:333
  133.2 9.3 %collective-permute-done.11.b = bf16[4,320,128]{2,1,0:T(8,128)(2,1)S(1)} collective-permute-done((bf16[4,320,128]{2,1,0:T(8,128)(2,1)S(1)}, bf16[4,320,128]{2,1,0:T(8,128)(2,1)S(1)}, u32[]{:S(2)}, u32[]{:S(2)}) %collective-permute-start.11) | collective-permute-done | bytes 327712 | tf_op jit(solution)/shard_map/ppermute | solution.py:333
  142.6 4.2 %collective-permute-start.12 = (bf16[4,320,128]{2,1,0:T(8,128)(2,1)S(1)}, bf16[4,320,128]{2,1,0:T(8,128)(2,1)S(1)}, u32[]{:S(2)}, u32[]{:S(2)}) collective-permute-start(bf16[4,320,128]{2,1,0:T(8,128)(2,1)S(1)} %add.11), channel_id=1, source_target_pairs={{0,128},{4,132},{8,136},{12,140},{16,144},{20,148},{24,152},{28,15... | collective-permute-start | bytes 983048 | tf_op jit(solution)/shard_map/ppermute | solution.py:329
  149.7 3.1 %final.3 = (bf16[160,2048]{1,0:T(8,128)(2,1)}, bf16[160,2048]{1,0:T(8,128)(2,1)}, bf16[160,2048]{1,0:T(8,128)(2,1)}) custom-call(s32[5]{0:T(128)S(1)} %copy-done.25, bf16[160,768]{1,0:T(8,128)(2,1)S(1)} %copy-done.14, bf16[160,768]{1,0:T(8,128)(2,1)S(1)} %copy-done.16, bf16[160,768]{1,0:T(8,128)(2,1)S(1)} %copy-done.18, bf16[6,320,128]{2,1,0:T(8,128)(2,1)} %arrived.13.home, ...), custom_call_target="tpu_custom_call" | custom-call | flops 1000 | bytes 1000 | tf_op jit(solution)/shard_map/final/pallas_call | solution.py:309
  152.7 11.6 %collective-permute-done.13.x = bf16[6,320,128]{2,1,0:T(8,128)(2,1)} collective-permute-done((bf16[6,320,128]{2,1,0:T(8,128)(2,1)S(1)}, bf16[6,320,128]{2,1,0:T(8,128)(2,1)}, u32[]{:S(2)}, u32[]{:S(2)}) %collective-permute-start.13) | collective-permute-done | bytes 491552 | tf_op jit(solution)/shard_map/ppermute | solution.py:329
  165.5 3.1 %final.4 = (bf16[160,2048]{1,0:T(8,128)(2,1)}, bf16[160,2048]{1,0:T(8,128)(2,1)}, bf16[160,2048]{1,0:T(8,128)(2,1)}) custom-call(s32[5]{0:T(128)S(1)} %copy-done.25, bf16[160,768]{1,0:T(8,128)(2,1)S(1)} %copy-done.8, bf16[160,768]{1,0:T(8,128)(2,1)S(1)} %copy-done.10, ...), custom_call_target="tpu_custom_call", output_to_operand_aliasing={{0}: (6, {}), {1}: (7, {}), {2}: (8, {})} | custom-call | flops 1000 | bytes 1000 | tf_op jit(solution)/shard_map/final/pallas_call | solution.py:309
  168.6 2.6 %collective-permute-done.12.x = bf16[4,320,128]{2,1,0:T(8,128)(2,1)S(1)} collective-permute-done((bf16[4,320,128]{2,1,0:T(8,128)(2,1)S(1)}, bf16[4,320,128]{2,1,0:T(8,128)(2,1)S(1)}, u32[]{:S(2)}, u32[]{:S(2)}) %collective-permute-start.12) | collective-permute-done | bytes 327712 | tf_op jit(solution)/shard_map/ppermute | solution.py:329
  (77 shorter events, 15.7 us)
Async XLA Ops:
  4.3 27.7 %collective-permute-start = (bf16[6,336,128]{2,1,0:T(8,128)(2,1)}, bf16[6,336,128]{2,1,0:T(8,128)(2,1)}, u32[]{:S(2)}, u32[]{:S(2)}) collective-permute-start(bf16[6,336,128]{2,1,0:T(8,128)(2,1)} %prep.4), channel_id=1, source_target_pairs={{0,384},{4,388},{8,392},{12,396},{16,400},{20,404},{24,408},{28,41... | collective-permute-start | bytes 1548296 | tf_op jit(solution)/shard_map/ppermute | solution.py:329
  20.0 24.5 %all-to-all-start = ((bf16[16,336,128]{2,1,0:T(8,128)(2,1)}), bf16[16,336,128]{2,1,0:T(8,128)(2,1)}, u32[]{:S(2)}, u32[]{:S(2)}) async-start(bf16[16,336,128]{2,1,0:T(8,128)(2,1)} %prep.7), calls=%async_computation | async-start | bytes 2752512 | tf_op jit(solution)/shard_map/all_to_all | solution.py:336
  31.9 23.6 %copy-start = (bf16[160,2048]{1,0:T(8,128)(2,1)S(1)}, bf16[160,2048]{1,0:T(8,128)(2,1)}, u32[]{:S(2)}) copy-start(bf16[160,2048]{1,0:T(8,128)(2,1)} %q.13) | copy-start | bytes 1966084
  31.9 23.6 %copy-start.1 = (bf16[160,2048]{1,0:T(8,128)(2,1)S(1)}, bf16[160,2048]{1,0:T(8,128)(2,1)}, u32[]{:S(2)}) copy-start(bf16[160,2048]{1,0:T(8,128)(2,1)} %g.13) | copy-start | bytes 1966084
  31.9 23.6 %copy-start.2 = (bf16[160,2048]{1,0:T(8,128)(2,1)S(1)}, bf16[160,2048]{1,0:T(8,128)(2,1)}, u32[]{:S(2)}) copy-start(bf16[160,2048]{1,0:T(8,128)(2,1)} %k.13) | copy-start | bytes 1966084
  31.9 23.6 %copy-start.3 = (bf16[160,2048]{1,0:T(8,128)(2,1)S(1)}, bf16[160,2048]{1,0:T(8,128)(2,1)}, u32[]{:S(2)}) copy-start(bf16[160,2048]{1,0:T(8,128)(2,1)} %v.13) | copy-start | bytes 1966084
  31.9 23.6 %copy-start.5 = (f32[16,160]{1,0:T(8,128)S(1)}, f32[16,160]{1,0:T(8,128)}, u32[]{:S(2)}) copy-start(f32[16,160]{1,0:T(8,128)} %lse.13) | copy-start | bytes 30724
  32.0 23.6 %copy-start.6 = (f32[16,160]{1,0:T(8,128)S(1)}, f32[16,160]{1,0:T(8,128)}, u32[]{:S(2)}) copy-start(f32[16,160]{1,0:T(8,128)} %delta.13) | copy-start | bytes 30724
  32.0 23.6 %copy-start.25 = (s32[5]{0:T(128)S(1)}, s32[5]{0:T(128)}, u32[]{:S(2)}) copy-start(s32[5]{0:T(128)} %stack.35.roles) | copy-start | bytes 64
  32.0 23.5 %collective-permute-start.2 = (bf16[6,336,128]{2,1,0:T(8,128)(2,1)}, bf16[6,336,128]{2,1,0:T(8,128)(2,1)}, u32[]{:S(2)}, u32[]{:S(2)}) collective-permute-start(bf16[6,336,128]{2,1,0:T(8,128)(2,1)} %arrived.8.one), channel_id=1, source_target_pairs={{4,0},{8,4},{12,8},{16,12},{20,16},{24,20},{28,24},{32,28},{36,32}... | collective-permute-start | bytes 1548296 | tf_op jit(solution)/shard_map/ppermute | solution.py:333
  36.8 43.2 %collective-permute-start.1 = (bf16[6,336,128]{2,1,0:T(8,128)(2,1)}, bf16[6,336,128]{2,1,0:T(8,128)(2,1)S(1)}, u32[]{:S(2)}, u32[]{:S(2)}) collective-permute-start(bf16[6,336,128]{2,1,0:T(8,128)(2,1)} %prep.6), channel_id=1, source_target_pairs={{0,384},{4,388},{8,392},{12,396},{16,400},{20,404},{24,408},{28,41... | collective-permute-start | bytes 1548296 | tf_op jit(solution)/shard_map/ppermute | solution.py:329
  45.4 31.3 %collective-permute-start.3 = (bf16[336,128]{1,0:T(8,128)(2,1)S(1)}, bf16[336,128]{1,0:T(8,128)(2,1)S(1)}, u32[]{:S(2)}, u32[]{:S(2)}) collective-permute-start(bf16[336,128]{1,0:T(8,128)(2,1)S(1)} %slice_bitcast_fusion), channel_id=1, source_target_pairs={{0,320},{4,324},{8,328},{12,332},{16,336},{20,340},{24,344},{28,34... | collective-permute-start | bytes 258056 | tf_op jit(solution)/shard_map/ppermute | solution.py:329
  60.4 19.6 %copy-start.15 = (bf16[160,768]{1,0:T(8,128)(2,1)}, bf16[160,768]{1,0:T(8,128)(2,1)S(1)}, u32[]{:S(2)}) copy-start(bf16[160,768]{1,0:T(8,128)(2,1)S(1)} %get-tuple-element.71.dk) | copy-start | bytes 737284
  60.4 19.6 %copy-start.17 = (bf16[160,768]{1,0:T(8,128)(2,1)}, bf16[160,768]{1,0:T(8,128)(2,1)S(1)}, u32[]{:S(2)}) copy-start(bf16[160,768]{1,0:T(8,128)(2,1)S(1)} %get-tuple-element.72.dv) | copy-start | bytes 737284
  60.4 28.6 %collective-permute-start.7 = (bf16[6,320,128]{2,1,0:T(8,128)(2,1)S(1)}, bf16[6,320,128]{2,1,0:T(8,128)(2,1)S(1)}, u32[]{:S(2)}, u32[]{:S(2)}) collective-permute-start(bf16[6,320,128]{2,1,0:T(8,128)(2,1)S(1)} %get-tuple-element.52), channel_id=1, source_target_pairs={{0,4},{4,8},{8,12},{12,16},{16,20},{20,24},{24,28},{28,32},{32,36}... | collective-permute-start | bytes 1474568 | tf_op jit(solution)/shard_map/ppermute | solution.py:333
  78.0 10.9 %collective-permute-start.6 = (bf16[320,128]{1,0:T(8,128)(2,1)S(1)}, bf16[320,128]{1,0:T(8,128)(2,1)S(1)}, u32[]{:S(2)}, u32[]{:S(2)}) collective-permute-start(bf16[320,128]{1,0:T(8,128)(2,1)S(1)} %get-tuple-element.48), channel_id=1, source_target_pairs={{0,192},{4,196},{8,200},{12,204},{16,208},{20,212},{24,216},{28,22... | collective-permute-start | bytes 245768 | tf_op jit(solution)/shard_map/ppermute | solution.py:329
  80.0 18.2 %collective-permute-start.5 = (bf16[6,336,128]{2,1,0:T(8,128)(2,1)S(1)}, bf16[6,336,128]{2,1,0:T(8,128)(2,1)}, u32[]{:S(2)}, u32[]{:S(2)}) collective-permute-start(bf16[6,336,128]{2,1,0:T(8,128)(2,1)S(1)} %arrived.10.one), channel_id=1, source_target_pairs={{4,0},{8,4},{12,8},{16,12},{20,16},{24,20},{28,24},{32,28},{36,32}... | collective-permute-start | bytes 1548296 | tf_op jit(solution)/shard_map/ppermute | solution.py:333
  82.4 32.4 %collective-permute-start.4 = (bf16[4,336,128]{2,1,0:T(8,128)(2,1)}, bf16[4,336,128]{2,1,0:T(8,128)(2,1)S(1)}, u32[]{:S(2)}, u32[]{:S(2)}) collective-permute-start(bf16[4,336,128]{2,1,0:T(8,128)(2,1)} %prep.5), channel_id=1, source_target_pairs={{0,384},{4,388},{8,392},{12,396},{16,400},{20,404},{24,408},{28,41... | collective-permute-start | bytes 1032200 | tf_op jit(solution)/shard_map/ppermute | solution.py:329
  89.9 38.5 %collective-permute-start.9 = (bf16[6,320,128]{2,1,0:T(8,128)(2,1)}, bf16[6,320,128]{2,1,0:T(8,128)(2,1)}, u32[]{:S(2)}, u32[]{:S(2)}) collective-permute-start(bf16[6,320,128]{2,1,0:T(8,128)(2,1)} %add.9), channel_id=1, source_target_pairs={{0,128},{4,132},{8,136},{12,140},{16,144},{20,148},{24,152},{28,15... | collective-permute-start | bytes 1474568 | tf_op jit(solution)/shard_map/ppermute | solution.py:329
  92.0 1.1 copy-start.4
  93.1 53.7 %all-to-all-start.1 = ((bf16[16,320,128]{2,1,0:T(8,128)(2,1)}), bf16[16,320,128]{2,1,0:T(8,128)(2,1)}, u32[]{:S(2)}, u32[]{:S(2)}) async-start(bf16[16,320,128]{2,1,0:T(8,128)(2,1)} %copy-done.4), calls=%async_computation.1 | async-start | bytes 2621440 | tf_op jit(solution)/shard_map/all_to_all | solution.py:336
  102.9 12.0 %copy-start.9 = (bf16[160,768]{1,0:T(8,128)(2,1)}, bf16[160,768]{1,0:T(8,128)(2,1)S(1)}, u32[]{:S(2)}) copy-start(bf16[160,768]{1,0:T(8,128)(2,1)S(1)} %get-tuple-element.68.dk) | copy-start | bytes 737284
  102.9 12.0 %copy-start.11 = (bf16[160,768]{1,0:T(8,128)(2,1)}, bf16[160,768]{1,0:T(8,128)(2,1)S(1)}, u32[]{:S(2)}) copy-start(bf16[160,768]{1,0:T(8,128)(2,1)S(1)} %get-tuple-element.69.dv) | copy-start | bytes 737284
  102.9 23.0 %collective-permute-start.10 = (bf16[6,320,128]{2,1,0:T(8,128)(2,1)S(1)}, bf16[6,320,128]{2,1,0:T(8,128)(2,1)S(1)}, u32[]{:S(2)}, u32[]{:S(2)}) collective-permute-start(bf16[6,320,128]{2,1,0:T(8,128)(2,1)S(1)} %get-tuple-element.59), channel_id=1, source_target_pairs={{0,4},{4,8},{8,12},{12,16},{16,20},{20,24},{24,28},{28,32},{32,36}... | collective-permute-start | bytes 1474568 | tf_op jit(solution)/shard_map/ppermute | solution.py:333
  114.9 13.6 %collective-permute-start.8 = (bf16[4,336,128]{2,1,0:T(8,128)(2,1)S(1)}, bf16[4,336,128]{2,1,0:T(8,128)(2,1)S(1)}, u32[]{:S(2)}, u32[]{:S(2)}) collective-permute-start(bf16[4,336,128]{2,1,0:T(8,128)(2,1)S(1)} %arrived.12.one), channel_id=1, source_target_pairs={{4,0},{8,4},{12,8},{16,12},{20,16},{24,20},{28,24},{32,28},{36,32}... | collective-permute-start | bytes 1032200 | tf_op jit(solution)/shard_map/ppermute | solution.py:333
  126.0 38.3 %collective-permute-start.13 = (bf16[6,320,128]{2,1,0:T(8,128)(2,1)S(1)}, bf16[6,320,128]{2,1,0:T(8,128)(2,1)}, u32[]{:S(2)}, u32[]{:S(2)}) collective-permute-start(bf16[6,320,128]{2,1,0:T(8,128)(2,1)S(1)} %add.10), channel_id=1, source_target_pairs={{0,128},{4,132},{8,136},{12,140},{16,144},{20,148},{24,152},{28,15... | collective-permute-start | bytes 1474568 | tf_op jit(solution)/shard_map/ppermute | solution.py:329
  131.1 11.5 %copy-start.19 = (bf16[160,512]{1,0:T(8,128)(2,1)}, bf16[160,512]{1,0:T(8,128)(2,1)S(1)}, u32[]{:S(2)}) copy-start(bf16[160,512]{1,0:T(8,128)(2,1)S(1)} %get-tuple-element.62.dq) | copy-start | bytes 491524
  131.1 11.5 %copy-start.21 = (bf16[160,512]{1,0:T(8,128)(2,1)}, bf16[160,512]{1,0:T(8,128)(2,1)S(1)}, u32[]{:S(2)}) copy-start(bf16[160,512]{1,0:T(8,128)(2,1)S(1)} %get-tuple-element.63.dk) | copy-start | bytes 491524
  131.1 11.5 %copy-start.23 = (bf16[160,512]{1,0:T(8,128)(2,1)}, bf16[160,512]{1,0:T(8,128)(2,1)S(1)}, u32[]{:S(2)}) copy-start(bf16[160,512]{1,0:T(8,128)(2,1)S(1)} %get-tuple-element.64.dv) | copy-start | bytes 491524
  131.1 11.4 %collective-permute-start.11 = (bf16[4,320,128]{2,1,0:T(8,128)(2,1)S(1)}, bf16[4,320,128]{2,1,0:T(8,128)(2,1)S(1)}, u32[]{:S(2)}, u32[]{:S(2)}) collective-permute-start(bf16[4,320,128]{2,1,0:T(8,128)(2,1)S(1)} %get-tuple-element.66), channel_id=1, source_target_pairs={{0,4},{4,8},{8,12},{12,16},{16,20},{20,24},{24,28},{28,32},{32,36}... | collective-permute-start | bytes 983048 | tf_op jit(solution)/shard_map/ppermute | solution.py:333
  142.6 28.6 %collective-permute-start.12 = (bf16[4,320,128]{2,1,0:T(8,128)(2,1)S(1)}, bf16[4,320,128]{2,1,0:T(8,128)(2,1)S(1)}, u32[]{:S(2)}, u32[]{:S(2)}) collective-permute-start(bf16[4,320,128]{2,1,0:T(8,128)(2,1)S(1)} %add.11), channel_id=1, source_target_pairs={{0,128},{4,132},{8,136},{12,140},{16,144},{20,148},{24,152},{28,15... | collective-permute-start | bytes 983048 | tf_op jit(solution)/shard_map/ppermute | solution.py:329
  164.3 1.2 copy-start.12
  (10 other events, 9.2 us)

commit v4 on v3

--- a/solution.py
+++ b/solution.py
@@ -341,11 +341,11 @@
     total = len(CHUNKS)
 
     sent = [None] * total
-    sent[0] = prep(firsts[0], CHUNKS[0], 0, roles, *inputs)
+    sent[0] = prep(firsts[0], CHUNKS[0], 0, roles, *inputs, unit=CHUNKS[0])
     roles1 = together(roles, sent[0])[0]
-    spread_in = spread(prep(0, HEADS, 2, roles1, *inputs, unit=4))
+    spread_in = spread(prep(0, HEADS, 2, roles1, *inputs, unit=8))
     for c in range(1, total):
-        sent[c] = prep(firsts[c], CHUNKS[c], 0, roles1, *inputs)
+        sent[c] = prep(firsts[c], CHUNKS[c], 0, roles1, *inputs, unit=CHUNKS[c])
 
     recv, near, own, summed, home = ([None] * total for _ in range(5))
     carried = carry_back = packed = None

time: 176 us -> 175 us (level)
  Pallas kernels: 33.7 us -> 31.2 us
  waiting for transfers between devices: 65.9 us -> 67.8 us
    ppermute x8, waiting for transfers between devices: 39.7 us -> 42.6 us  [ring(): return lax.ppermute(x, 'seq', [(i, (i + by) % count) for i in range(count)])]
    pallas_call x4, Pallas kernels: 12.2 us -> 9.8 us  [prep(): call(functools.partial(prep_kernel, first, role_at, unit), 'prep', grid=(...]
where the time goes in v4:
time: 175 us; the launch traced here: 174 us
  waiting for transfers between devices  67.8 us (39%)
  starting transfers between devices  64.3 us (37%)
  Pallas kernels  31.2 us (18%)
  local copies, waits for them, and re-layouts  9.14 us (5%)
    ppermute x8, waiting for transfers between devices, ring(): return lax.ppermute(x, 'seq', [(i, (i + by) % count) for i in range(count)])  42.6 us
    ppermute x8, starting transfers between devices, ring(): return lax.ppermute(x, 'seq', [(i, (i + by) % count) for i in range(count)])  35.7 us
    ppermute x6, waiting for transfers between devices, beside(): return lax.ppermute(x, 'seq', pairs)  25.2 us
    ppermute x6, starting transfers between devices, beside(): return lax.ppermute(x, 'seq', pairs)  16.6 us
    all_to_all x2, starting transfers between devices, spread(): return lax.all_to_all(x, 'seq', 0, 0, axis_index_groups=groups, tiled=True)  12 us
    pallas_call x3, Pallas kernels, edges(): call(functools.partial(edges_kernel, first), 'edges', limit=24 * 1024 * 1...  10.7 us
    pallas_call x4, Pallas kernels, prep(): call(functools.partial(prep_kernel, first, role_at, unit), 'prep', grid=(...  9.8 us
    pallas_call x3, Pallas kernels, final(): call(final_kernel, 'final', limit=24 * 1024 * 1024, grid=(count // UNIT,)...  8.09 us
  transfers between devices with their start and end apart: 16, of which 9 were waited for; matrix products, arithmetic and copies ran while one was open for 1% of the time, Pallas kernels for 16%

profile of v4, /device:TPU:5, one launch (start us, length us, event | category | flops | bytes accessed | tf_op | source)
XLA Modules:
  0.0 173.5 jit_solution(7995859180865033017)
XLA Ops:
  1.3 2.4 %prep.4 = bf16[6,336,128]{2,1,0:T(8,128)(2,1)} custom-call(s32[5]{0:T(128)} %stack.35.roles, bf16[160,2048]{1,0:T(8,128)(2,1)} %q.13, bf16[160,2048]{1,0:T(8,128)(2,1)} %g.13, bf16[160,2048]{1,0:T(8,128)(2,1)} %k.13, bf16[160,2048]{1,0:T(8,128)(2,1)} %v.13, f32[16,160]{1,0:T(8,128)} %lse.13, f32[16,160]{1,0:T(8,128)} %delta.13), custom_call_target="tpu_custom_call" | custom-call | flops 1000 | bytes 1000 | tf_op jit(solution)/shard_map/prep/pallas_call | solution.py:134
  3.6 11.5 %collective-permute-start = (bf16[6,336,128]{2,1,0:T(8,128)(2,1)}, bf16[6,336,128]{2,1,0:T(8,128)(2,1)}, u32[]{:S(2)}, u32[]{:S(2)}) collective-permute-start(bf16[6,336,128]{2,1,0:T(8,128)(2,1)} %prep.4), channel_id=1, source_target_pairs={{0,384},{4,388},{8,392},{12,396},{16,400},{20,404},{24,408},{28,41... | collective-permute-start | bytes 1548296 | tf_op jit(solution)/shard_map/ppermute | solution.py:329
  15.1 3.0 %prep.7 = bf16[16,336,128]{2,1,0:T(8,128)(2,1)} custom-call(s32[5]{0:T(128)} %stack.35.roles, bf16[160,2048]{1,0:T(8,128)(2,1)} %q.13, bf16[160,2048]{1,0:T(8,128)(2,1)} %g.13, bf16[160,2048]{1,0:T(8,128)(2,1)} %k.13, bf16[160,2048]{1,0:T(8,128)(2,1)} %v.13, f32[16,160]{1,0:T(8,128)} %lse.13, f32[16,160]{1,0:T(8,128)} %delta.13), custom_call_target="tpu_custom_call" | custom-call | flops 1000 | bytes 1000 | tf_op jit(solution)/shard_map/prep/pallas_call | solution.py:134
  18.1 6.9 %all-to-all-start = ((bf16[16,336,128]{2,1,0:T(8,128)(2,1)}), bf16[16,336,128]{2,1,0:T(8,128)(2,1)}, u32[]{:S(2)}, u32[]{:S(2)}) async-start(bf16[16,336,128]{2,1,0:T(8,128)(2,1)} %prep.7), calls=%async_computation | async-start | bytes 2752512 | tf_op jit(solution)/shard_map/all_to_all | solution.py:336
  25.0 2.4 %prep.6 = bf16[6,336,128]{2,1,0:T(8,128)(2,1)} custom-call(s32[5]{0:T(128)} %stack.35.roles, bf16[160,2048]{1,0:T(8,128)(2,1)} %q.13, bf16[160,2048]{1,0:T(8,128)(2,1)} %g.13, bf16[160,2048]{1,0:T(8,128)(2,1)} %k.13, bf16[160,2048]{1,0:T(8,128)(2,1)} %v.13, f32[16,160]{1,0:T(8,128)} %lse.13, f32[16,160]{1,0:T(8,128)} %delta.13), custom_call_target="tpu_custom_call" | custom-call | flops 1000 | bytes 1000 | tf_op jit(solution)/shard_map/prep/pallas_call | solution.py:134
  27.4 2.1 %prep.5 = bf16[4,336,128]{2,1,0:T(8,128)(2,1)} custom-call(s32[5]{0:T(128)} %stack.35.roles, bf16[160,2048]{1,0:T(8,128)(2,1)} %q.13, bf16[160,2048]{1,0:T(8,128)(2,1)} %g.13, bf16[160,2048]{1,0:T(8,128)(2,1)} %k.13, bf16[160,2048]{1,0:T(8,128)(2,1)} %v.13, f32[16,160]{1,0:T(8,128)} %lse.13, f32[16,160]{1,0:T(8,128)} %delta.13), custom_call_target="tpu_custom_call" | custom-call | flops 1000 | bytes 1000 | tf_op jit(solution)/shard_map/prep/pallas_call | solution.py:134
  31.3 4.6 %collective-permute-start.2 = (bf16[6,336,128]{2,1,0:T(8,128)(2,1)}, bf16[6,336,128]{2,1,0:T(8,128)(2,1)}, u32[]{:S(2)}, u32[]{:S(2)}) collective-permute-start(bf16[6,336,128]{2,1,0:T(8,128)(2,1)} %arrived.8.one), channel_id=1, source_target_pairs={{4,0},{8,4},{12,8},{16,12},{20,16},{24,20},{28,24},{32,28},{36,32}... | collective-permute-start | bytes 1548296 | tf_op jit(solution)/shard_map/ppermute | solution.py:333
  35.9 7.8 %collective-permute-start.1 = (bf16[6,336,128]{2,1,0:T(8,128)(2,1)}, bf16[6,336,128]{2,1,0:T(8,128)(2,1)S(1)}, u32[]{:S(2)}, u32[]{:S(2)}) collective-permute-start(bf16[6,336,128]{2,1,0:T(8,128)(2,1)} %prep.6), channel_id=1, source_target_pairs={{0,384},{4,388},{8,392},{12,396},{16,400},{20,404},{24,408},{28,41... | collective-permute-start | bytes 1548296 | tf_op jit(solution)/shard_map/ppermute | solution.py:329
  46.6 7.2 %collective-permute-done.2.two = bf16[6,336,128]{2,1,0:T(8,128)(2,1)} collective-permute-done((bf16[6,336,128]{2,1,0:T(8,128)(2,1)}, bf16[6,336,128]{2,1,0:T(8,128)(2,1)}, u32[]{:S(2)}, u32[]{:S(2)}) %collective-permute-start.2) | collective-permute-done | bytes 516128 | tf_op jit(solution)/shard_map/ppermute | solution.py:333
  53.8 4.1 %edges.3 = (bf16[6,320,128]{2,1,0:T(8,128)(2,1)S(1)}, bf16[6,320,128]{2,1,0:T(8,128)(2,1)S(1)}, bf16[160,768]{1,0:T(8,128)(2,1)S(1)}, bf16[160,768]{1,0:T(8,128)(2,1)S(1)}, bf16[160,768]{1,0:T(8,128)(2,1)S(1)}) custom-call(s32[5]{0:T(128)S(1)} %copy-done.25, bf16[160,2048]{1,0:T(8,128)(2,1)S(1)} %copy-done, bf16[160,2048]{1,0:T(8,128)(2,1)S(1)} %copy-done.1, ...), custom_call_target="tpu_custom_call" | custom-call | flops 1000 | bytes 1000 | tf_op jit(solution)/shard_map/edges/pallas_call | solution.py:197
  58.7 2.1 %collective-permute-start.7 = (bf16[6,320,128]{2,1,0:T(8,128)(2,1)S(1)}, bf16[6,320,128]{2,1,0:T(8,128)(2,1)S(1)}, u32[]{:S(2)}, u32[]{:S(2)}) collective-permute-start(bf16[6,320,128]{2,1,0:T(8,128)(2,1)S(1)} %get-tuple-element.52), channel_id=1, source_target_pairs={{0,4},{4,8},{8,12},{12,16},{16,20},{20,24},{24,28},{28,32},{32,36}... | collective-permute-start | bytes 1474568 | tf_op jit(solution)/shard_map/ppermute | solution.py:333
  60.8 15.2 %collective-permute-done.3.x = bf16[336,128]{1,0:T(8,128)(2,1)S(1)} collective-permute-done((bf16[336,128]{1,0:T(8,128)(2,1)S(1)}, bf16[336,128]{1,0:T(8,128)(2,1)S(1)}, u32[]{:S(2)}, u32[]{:S(2)}) %collective-permute-start.3) | collective-permute-done | bytes 86048 | tf_op jit(solution)/shard_map/ppermute | solution.py:329
  77.3 1.9 %collective-permute-start.6 = (bf16[320,128]{1,0:T(8,128)(2,1)S(1)}, bf16[320,128]{1,0:T(8,128)(2,1)S(1)}, u32[]{:S(2)}, u32[]{:S(2)}) collective-permute-start(bf16[320,128]{1,0:T(8,128)(2,1)S(1)} %get-tuple-element.48), channel_id=1, source_target_pairs={{0,192},{4,196},{8,200},{12,204},{16,208},{20,212},{24,216},{28,22... | collective-permute-start | bytes 245768 | tf_op jit(solution)/shard_map/ppermute | solution.py:329
  79.3 2.4 %collective-permute-start.5 = (bf16[6,336,128]{2,1,0:T(8,128)(2,1)S(1)}, bf16[6,336,128]{2,1,0:T(8,128)(2,1)}, u32[]{:S(2)}, u32[]{:S(2)}) collective-permute-start(bf16[6,336,128]{2,1,0:T(8,128)(2,1)S(1)} %arrived.10.one), channel_id=1, source_target_pairs={{4,0},{8,4},{12,8},{16,12},{20,16},{24,20},{28,24},{32,28},{36,32}... | collective-permute-start | bytes 1548296 | tf_op jit(solution)/shard_map/ppermute | solution.py:333
  81.7 4.1 %collective-permute-start.4 = (bf16[4,336,128]{2,1,0:T(8,128)(2,1)}, bf16[4,336,128]{2,1,0:T(8,128)(2,1)S(1)}, u32[]{:S(2)}, u32[]{:S(2)}) collective-permute-start(bf16[4,336,128]{2,1,0:T(8,128)(2,1)} %prep.5), channel_id=1, source_target_pairs={{0,384},{4,388},{8,392},{12,396},{16,400},{20,404},{24,408},{28,41... | collective-permute-start | bytes 1032200 | tf_op jit(solution)/shard_map/ppermute | solution.py:329
  85.8 2.5 %collective-permute-done.6.x = bf16[320,128]{1,0:T(8,128)(2,1)S(1)} collective-permute-done((bf16[320,128]{1,0:T(8,128)(2,1)S(1)}, bf16[320,128]{1,0:T(8,128)(2,1)S(1)}, u32[]{:S(2)}, u32[]{:S(2)}) %collective-permute-start.6) | collective-permute-done | bytes 81952 | tf_op jit(solution)/shard_map/ppermute | solution.py:329
  89.2 1.9 %collective-permute-start.9 = (bf16[6,320,128]{2,1,0:T(8,128)(2,1)}, bf16[6,320,128]{2,1,0:T(8,128)(2,1)}, u32[]{:S(2)}, u32[]{:S(2)}) collective-permute-start(bf16[6,320,128]{2,1,0:T(8,128)(2,1)} %add.9), channel_id=1, source_target_pairs={{0,128},{4,132},{8,136},{12,140},{16,144},{20,148},{24,152},{28,15... | collective-permute-start | bytes 1474568 | tf_op jit(solution)/shard_map/ppermute | solution.py:329
  92.4 5.1 %all-to-all-start.1 = ((bf16[16,320,128]{2,1,0:T(8,128)(2,1)}), bf16[16,320,128]{2,1,0:T(8,128)(2,1)}, u32[]{:S(2)}, u32[]{:S(2)}) async-start(bf16[16,320,128]{2,1,0:T(8,128)(2,1)} %copy-done.4), calls=%async_computation.1 | async-start | bytes 2621440 | tf_op jit(solution)/shard_map/all_to_all | solution.py:336
  97.5 4.0 %edges.4 = (bf16[6,320,128]{2,1,0:T(8,128)(2,1)S(1)}, bf16[6,320,128]{2,1,0:T(8,128)(2,1)S(1)}, bf16[160,768]{1,0:T(8,128)(2,1)S(1)}, bf16[160,768]{1,0:T(8,128)(2,1)S(1)}, bf16[160,768]{1,0:T(8,128)(2,1)S(1)}) custom-call(s32[5]{0:T(128)S(1)} %copy-done.25, bf16[160,2048]{1,0:T(8,128)(2,1)S(1)} %copy-done, bf16[160,2048]{1,0:T(8,128)(2,1)S(1)} %copy-done.1, ...), custom_call_target="tpu_custom_call" | custom-call | flops 1000 | bytes 1000 | tf_op jit(solution)/shard_map/edges/pallas_call | solution.py:197
  102.2 3.1 %collective-permute-start.10 = (bf16[6,320,128]{2,1,0:T(8,128)(2,1)S(1)}, bf16[6,320,128]{2,1,0:T(8,128)(2,1)S(1)}, u32[]{:S(2)}, u32[]{:S(2)}) collective-permute-start(bf16[6,320,128]{2,1,0:T(8,128)(2,1)S(1)} %get-tuple-element.59), channel_id=1, source_target_pairs={{0,4},{4,8},{8,12},{12,16},{16,20},{20,24},{24,28},{28,32},{32,36}... | collective-permute-start | bytes 1474568 | tf_op jit(solution)/shard_map/ppermute | solution.py:333
  105.3 8.9 %collective-permute-done.4.x = bf16[4,336,128]{2,1,0:T(8,128)(2,1)S(1)} collective-permute-done((bf16[4,336,128]{2,1,0:T(8,128)(2,1)}, bf16[4,336,128]{2,1,0:T(8,128)(2,1)S(1)}, u32[]{:S(2)}, u32[]{:S(2)}) %collective-permute-start.4) | collective-permute-done | bytes 344096 | tf_op jit(solution)/shard_map/ppermute | solution.py:329
  114.2 2.3 %collective-permute-start.8 = (bf16[4,336,128]{2,1,0:T(8,128)(2,1)S(1)}, bf16[4,336,128]{2,1,0:T(8,128)(2,1)S(1)}, u32[]{:S(2)}, u32[]{:S(2)}) collective-permute-start(bf16[4,336,128]{2,1,0:T(8,128)(2,1)S(1)} %arrived.12.one), channel_id=1, source_target_pairs={{4,0},{8,4},{12,8},{16,12},{20,16},{24,20},{28,24},{32,28},{36,32}... | collective-permute-start | bytes 1032200 | tf_op jit(solution)/shard_map/ppermute | solution.py:333
  116.5 8.7 %collective-permute-done.10.b = bf16[6,320,128]{2,1,0:T(8,128)(2,1)S(1)} collective-permute-done((bf16[6,320,128]{2,1,0:T(8,128)(2,1)S(1)}, bf16[6,320,128]{2,1,0:T(8,128)(2,1)S(1)}, u32[]{:S(2)}, u32[]{:S(2)}) %collective-permute-start.10) | collective-permute-done | bytes 491552 | tf_op jit(solution)/shard_map/ppermute | solution.py:333
  125.3 2.4 %collective-permute-start.13 = (bf16[6,320,128]{2,1,0:T(8,128)(2,1)S(1)}, bf16[6,320,128]{2,1,0:T(8,128)(2,1)}, u32[]{:S(2)}, u32[]{:S(2)}) collective-permute-start(bf16[6,320,128]{2,1,0:T(8,128)(2,1)S(1)} %add.10), channel_id=1, source_target_pairs={{0,128},{4,132},{8,136},{12,140},{16,144},{20,148},{24,152},{28,15... | collective-permute-start | bytes 1474568 | tf_op jit(solution)/shard_map/ppermute | solution.py:329
  127.7 2.6 %edges.5 = (bf16[4,320,128]{2,1,0:T(8,128)(2,1)S(1)}, bf16[4,320,128]{2,1,0:T(8,128)(2,1)S(1)}, bf16[160,512]{1,0:T(8,128)(2,1)S(1)}, bf16[160,512]{1,0:T(8,128)(2,1)S(1)}, bf16[160,512]{1,0:T(8,128)(2,1)S(1)}) custom-call(s32[5]{0:T(128)S(1)} %copy-done.25, bf16[160,2048]{1,0:T(8,128)(2,1)S(1)} %copy-done, bf16[160,2048]{1,0:T(8,128)(2,1)S(1)} %copy-done.1, ...), custom_call_target="tpu_custom_call" | custom-call | flops 1000 | bytes 1000 | tf_op jit(solution)/shard_map/edges/pallas_call | solution.py:197
  130.4 2.1 %collective-permute-start.11 = (bf16[4,320,128]{2,1,0:T(8,128)(2,1)S(1)}, bf16[4,320,128]{2,1,0:T(8,128)(2,1)S(1)}, u32[]{:S(2)}, u32[]{:S(2)}) collective-permute-start(bf16[4,320,128]{2,1,0:T(8,128)(2,1)S(1)} %get-tuple-element.66), channel_id=1, source_target_pairs={{0,4},{4,8},{8,12},{12,16},{16,20},{20,24},{24,28},{28,32},{32,36}... | collective-permute-start | bytes 983048 | tf_op jit(solution)/shard_map/ppermute | solution.py:333
  132.5 9.3 %collective-permute-done.11.b = bf16[4,320,128]{2,1,0:T(8,128)(2,1)S(1)} collective-permute-done((bf16[4,320,128]{2,1,0:T(8,128)(2,1)S(1)}, bf16[4,320,128]{2,1,0:T(8,128)(2,1)S(1)}, u32[]{:S(2)}, u32[]{:S(2)}) %collective-permute-start.11) | collective-permute-done | bytes 327712 | tf_op jit(solution)/shard_map/ppermute | solution.py:333
  141.9 4.2 %collective-permute-start.12 = (bf16[4,320,128]{2,1,0:T(8,128)(2,1)S(1)}, bf16[4,320,128]{2,1,0:T(8,128)(2,1)S(1)}, u32[]{:S(2)}, u32[]{:S(2)}) collective-permute-start(bf16[4,320,128]{2,1,0:T(8,128)(2,1)S(1)} %add.11), channel_id=1, source_target_pairs={{0,128},{4,132},{8,136},{12,140},{16,144},{20,148},{24,152},{28,15... | collective-permute-start | bytes 983048 | tf_op jit(solution)/shard_map/ppermute | solution.py:329
  148.9 3.1 %final.3 = (bf16[160,2048]{1,0:T(8,128)(2,1)}, bf16[160,2048]{1,0:T(8,128)(2,1)}, bf16[160,2048]{1,0:T(8,128)(2,1)}) custom-call(s32[5]{0:T(128)S(1)} %copy-done.25, bf16[160,768]{1,0:T(8,128)(2,1)S(1)} %copy-done.14, bf16[160,768]{1,0:T(8,128)(2,1)S(1)} %copy-done.16, bf16[160,768]{1,0:T(8,128)(2,1)S(1)} %copy-done.18, bf16[6,320,128]{2,1,0:T(8,128)(2,1)} %arrived.13.home, ...), custom_call_target="tpu_custom_call" | custom-call | flops 1000 | bytes 1000 | tf_op jit(solution)/shard_map/final/pallas_call | solution.py:309
  152.0 11.6 %collective-permute-done.13.x = bf16[6,320,128]{2,1,0:T(8,128)(2,1)} collective-permute-done((bf16[6,320,128]{2,1,0:T(8,128)(2,1)S(1)}, bf16[6,320,128]{2,1,0:T(8,128)(2,1)}, u32[]{:S(2)}, u32[]{:S(2)}) %collective-permute-start.13) | collective-permute-done | bytes 491552 | tf_op jit(solution)/shard_map/ppermute | solution.py:329
  164.8 3.1 %final.4 = (bf16[160,2048]{1,0:T(8,128)(2,1)}, bf16[160,2048]{1,0:T(8,128)(2,1)}, bf16[160,2048]{1,0:T(8,128)(2,1)}) custom-call(s32[5]{0:T(128)S(1)} %copy-done.25, bf16[160,768]{1,0:T(8,128)(2,1)S(1)} %copy-done.8, bf16[160,768]{1,0:T(8,128)(2,1)S(1)} %copy-done.10, ...), custom_call_target="tpu_custom_call", output_to_operand_aliasing={{0}: (6, {}), {1}: (7, {}), {2}: (8, {})} | custom-call | flops 1000 | bytes 1000 | tf_op jit(solution)/shard_map/final/pallas_call | solution.py:309
  167.9 2.6 %collective-permute-done.12.x = bf16[4,320,128]{2,1,0:T(8,128)(2,1)S(1)} collective-permute-done((bf16[4,320,128]{2,1,0:T(8,128)(2,1)S(1)}, bf16[4,320,128]{2,1,0:T(8,128)(2,1)S(1)}, u32[]{:S(2)}, u32[]{:S(2)}) %collective-permute-start.12) | collective-permute-done | bytes 327712 | tf_op jit(solution)/shard_map/ppermute | solution.py:329
  (77 shorter events, 17.4 us)
Async XLA Ops:
  3.6 27.7 %collective-permute-start = (bf16[6,336,128]{2,1,0:T(8,128)(2,1)}, bf16[6,336,128]{2,1,0:T(8,128)(2,1)}, u32[]{:S(2)}, u32[]{:S(2)}) collective-permute-start(bf16[6,336,128]{2,1,0:T(8,128)(2,1)} %prep.4), channel_id=1, source_target_pairs={{0,384},{4,388},{8,392},{12,396},{16,400},{20,404},{24,408},{28,41... | collective-permute-start | bytes 1548296 | tf_op jit(solution)/shard_map/ppermute | solution.py:329
  18.1 25.7 %all-to-all-start = ((bf16[16,336,128]{2,1,0:T(8,128)(2,1)}), bf16[16,336,128]{2,1,0:T(8,128)(2,1)}, u32[]{:S(2)}, u32[]{:S(2)}) async-start(bf16[16,336,128]{2,1,0:T(8,128)(2,1)} %prep.7), calls=%async_computation | async-start | bytes 2752512 | tf_op jit(solution)/shard_map/all_to_all | solution.py:336
  29.5 24.3 %copy-start = (bf16[160,2048]{1,0:T(8,128)(2,1)S(1)}, bf16[160,2048]{1,0:T(8,128)(2,1)}, u32[]{:S(2)}) copy-start(bf16[160,2048]{1,0:T(8,128)(2,1)} %q.13) | copy-start | bytes 1966084
  29.5 24.3 %copy-start.1 = (bf16[160,2048]{1,0:T(8,128)(2,1)S(1)}, bf16[160,2048]{1,0:T(8,128)(2,1)}, u32[]{:S(2)}) copy-start(bf16[160,2048]{1,0:T(8,128)(2,1)} %g.13) | copy-start | bytes 1966084
  29.5 24.3 %copy-start.2 = (bf16[160,2048]{1,0:T(8,128)(2,1)S(1)}, bf16[160,2048]{1,0:T(8,128)(2,1)}, u32[]{:S(2)}) copy-start(bf16[160,2048]{1,0:T(8,128)(2,1)} %k.13) | copy-start | bytes 1966084
  29.5 24.3 %copy-start.3 = (bf16[160,2048]{1,0:T(8,128)(2,1)S(1)}, bf16[160,2048]{1,0:T(8,128)(2,1)}, u32[]{:S(2)}) copy-start(bf16[160,2048]{1,0:T(8,128)(2,1)} %v.13) | copy-start | bytes 1966084
  29.5 24.3 %copy-start.5 = (f32[16,160]{1,0:T(8,128)S(1)}, f32[16,160]{1,0:T(8,128)}, u32[]{:S(2)}) copy-start(f32[16,160]{1,0:T(8,128)} %lse.13) | copy-start | bytes 30724
  29.5 24.3 %copy-start.6 = (f32[16,160]{1,0:T(8,128)S(1)}, f32[16,160]{1,0:T(8,128)}, u32[]{:S(2)}) copy-start(f32[16,160]{1,0:T(8,128)} %delta.13) | copy-start | bytes 30724
  29.5 24.3 %copy-start.25 = (s32[5]{0:T(128)S(1)}, s32[5]{0:T(128)}, u32[]{:S(2)}) copy-start(s32[5]{0:T(128)} %stack.35.roles) | copy-start | bytes 64
  31.3 22.5 %collective-permute-start.2 = (bf16[6,336,128]{2,1,0:T(8,128)(2,1)}, bf16[6,336,128]{2,1,0:T(8,128)(2,1)}, u32[]{:S(2)}, u32[]{:S(2)}) collective-permute-start(bf16[6,336,128]{2,1,0:T(8,128)(2,1)} %arrived.8.one), channel_id=1, source_target_pairs={{4,0},{8,4},{12,8},{16,12},{20,16},{24,20},{28,24},{32,28},{36,32}... | collective-permute-start | bytes 1548296 | tf_op jit(solution)/shard_map/ppermute | solution.py:333
  35.9 43.3 %collective-permute-start.1 = (bf16[6,336,128]{2,1,0:T(8,128)(2,1)}, bf16[6,336,128]{2,1,0:T(8,128)(2,1)S(1)}, u32[]{:S(2)}, u32[]{:S(2)}) collective-permute-start(bf16[6,336,128]{2,1,0:T(8,128)(2,1)} %prep.6), channel_id=1, source_target_pairs={{0,384},{4,388},{8,392},{12,396},{16,400},{20,404},{24,408},{28,41... | collective-permute-start | bytes 1548296 | tf_op jit(solution)/shard_map/ppermute | solution.py:329
  44.7 31.3 %collective-permute-start.3 = (bf16[336,128]{1,0:T(8,128)(2,1)S(1)}, bf16[336,128]{1,0:T(8,128)(2,1)S(1)}, u32[]{:S(2)}, u32[]{:S(2)}) collective-permute-start(bf16[336,128]{1,0:T(8,128)(2,1)S(1)} %slice_bitcast_fusion), channel_id=1, source_target_pairs={{0,320},{4,324},{8,328},{12,332},{16,336},{20,340},{24,344},{28,34... | collective-permute-start | bytes 258056 | tf_op jit(solution)/shard_map/ppermute | solution.py:329
  58.7 20.6 %copy-start.15 = (bf16[160,768]{1,0:T(8,128)(2,1)}, bf16[160,768]{1,0:T(8,128)(2,1)S(1)}, u32[]{:S(2)}) copy-start(bf16[160,768]{1,0:T(8,128)(2,1)S(1)} %get-tuple-element.71.dk) | copy-start | bytes 737284
  58.7 20.6 %copy-start.17 = (bf16[160,768]{1,0:T(8,128)(2,1)}, bf16[160,768]{1,0:T(8,128)(2,1)S(1)}, u32[]{:S(2)}) copy-start(bf16[160,768]{1,0:T(8,128)(2,1)S(1)} %get-tuple-element.72.dv) | copy-start | bytes 737284
  58.7 29.6 %collective-permute-start.7 = (bf16[6,320,128]{2,1,0:T(8,128)(2,1)S(1)}, bf16[6,320,128]{2,1,0:T(8,128)(2,1)S(1)}, u32[]{:S(2)}, u32[]{:S(2)}) collective-permute-start(bf16[6,320,128]{2,1,0:T(8,128)(2,1)S(1)} %get-tuple-element.52), channel_id=1, source_target_pairs={{0,4},{4,8},{8,12},{12,16},{16,20},{20,24},{24,28},{28,32},{32,36}... | collective-permute-start | bytes 1474568 | tf_op jit(solution)/shard_map/ppermute | solution.py:333
  77.3 10.9 %collective-permute-start.6 = (bf16[320,128]{1,0:T(8,128)(2,1)S(1)}, bf16[320,128]{1,0:T(8,128)(2,1)S(1)}, u32[]{:S(2)}, u32[]{:S(2)}) collective-permute-start(bf16[320,128]{1,0:T(8,128)(2,1)S(1)} %get-tuple-element.48), channel_id=1, source_target_pairs={{0,192},{4,196},{8,200},{12,204},{16,208},{20,212},{24,216},{28,22... | collective-permute-start | bytes 245768 | tf_op jit(solution)/shard_map/ppermute | solution.py:329
  79.3 18.2 %collective-permute-start.5 = (bf16[6,336,128]{2,1,0:T(8,128)(2,1)S(1)}, bf16[6,336,128]{2,1,0:T(8,128)(2,1)}, u32[]{:S(2)}, u32[]{:S(2)}) collective-permute-start(bf16[6,336,128]{2,1,0:T(8,128)(2,1)S(1)} %arrived.10.one), channel_id=1, source_target_pairs={{4,0},{8,4},{12,8},{16,12},{20,16},{24,20},{28,24},{32,28},{36,32}... | collective-permute-start | bytes 1548296 | tf_op jit(solution)/shard_map/ppermute | solution.py:333
  81.7 32.4 %collective-permute-start.4 = (bf16[4,336,128]{2,1,0:T(8,128)(2,1)}, bf16[4,336,128]{2,1,0:T(8,128)(2,1)S(1)}, u32[]{:S(2)}, u32[]{:S(2)}) collective-permute-start(bf16[4,336,128]{2,1,0:T(8,128)(2,1)} %prep.5), channel_id=1, source_target_pairs={{0,384},{4,388},{8,392},{12,396},{16,400},{20,404},{24,408},{28,41... | collective-permute-start | bytes 1032200 | tf_op jit(solution)/shard_map/ppermute | solution.py:329
  89.2 38.5 %collective-permute-start.9 = (bf16[6,320,128]{2,1,0:T(8,128)(2,1)}, bf16[6,320,128]{2,1,0:T(8,128)(2,1)}, u32[]{:S(2)}, u32[]{:S(2)}) collective-permute-start(bf16[6,320,128]{2,1,0:T(8,128)(2,1)} %add.9), channel_id=1, source_target_pairs={{0,128},{4,132},{8,136},{12,140},{16,144},{20,148},{24,152},{28,15... | collective-permute-start | bytes 1474568 | tf_op jit(solution)/shard_map/ppermute | solution.py:329
  91.3 1.1 copy-start.4
  92.4 53.7 %all-to-all-start.1 = ((bf16[16,320,128]{2,1,0:T(8,128)(2,1)}), bf16[16,320,128]{2,1,0:T(8,128)(2,1)}, u32[]{:S(2)}, u32[]{:S(2)}) async-start(bf16[16,320,128]{2,1,0:T(8,128)(2,1)} %copy-done.4), calls=%async_computation.1 | async-start | bytes 2621440 | tf_op jit(solution)/shard_map/all_to_all | solution.py:336
  102.2 12.0 %copy-start.9 = (bf16[160,768]{1,0:T(8,128)(2,1)}, bf16[160,768]{1,0:T(8,128)(2,1)S(1)}, u32[]{:S(2)}) copy-start(bf16[160,768]{1,0:T(8,128)(2,1)S(1)} %get-tuple-element.68.dk) | copy-start | bytes 737284
  102.2 12.0 %copy-start.11 = (bf16[160,768]{1,0:T(8,128)(2,1)}, bf16[160,768]{1,0:T(8,128)(2,1)S(1)}, u32[]{:S(2)}) copy-start(bf16[160,768]{1,0:T(8,128)(2,1)S(1)} %get-tuple-element.69.dv) | copy-start | bytes 737284
  102.2 23.0 %collective-permute-start.10 = (bf16[6,320,128]{2,1,0:T(8,128)(2,1)S(1)}, bf16[6,320,128]{2,1,0:T(8,128)(2,1)S(1)}, u32[]{:S(2)}, u32[]{:S(2)}) collective-permute-start(bf16[6,320,128]{2,1,0:T(8,128)(2,1)S(1)} %get-tuple-element.59), channel_id=1, source_target_pairs={{0,4},{4,8},{8,12},{12,16},{16,20},{20,24},{24,28},{28,32},{32,36}... | collective-permute-start | bytes 1474568 | tf_op jit(solution)/shard_map/ppermute | solution.py:333
  114.2 13.6 %collective-permute-start.8 = (bf16[4,336,128]{2,1,0:T(8,128)(2,1)S(1)}, bf16[4,336,128]{2,1,0:T(8,128)(2,1)S(1)}, u32[]{:S(2)}, u32[]{:S(2)}) collective-permute-start(bf16[4,336,128]{2,1,0:T(8,128)(2,1)S(1)} %arrived.12.one), channel_id=1, source_target_pairs={{4,0},{8,4},{12,8},{16,12},{20,16},{24,20},{28,24},{32,28},{36,32}... | collective-permute-start | bytes 1032200 | tf_op jit(solution)/shard_map/ppermute | solution.py:333
  125.3 38.3 %collective-permute-start.13 = (bf16[6,320,128]{2,1,0:T(8,128)(2,1)S(1)}, bf16[6,320,128]{2,1,0:T(8,128)(2,1)}, u32[]{:S(2)}, u32[]{:S(2)}) collective-permute-start(bf16[6,320,128]{2,1,0:T(8,128)(2,1)S(1)} %add.10), channel_id=1, source_target_pairs={{0,128},{4,132},{8,136},{12,140},{16,144},{20,148},{24,152},{28,15... | collective-permute-start | bytes 1474568 | tf_op jit(solution)/shard_map/ppermute | solution.py:329
  130.3 11.5 %copy-start.19 = (bf16[160,512]{1,0:T(8,128)(2,1)}, bf16[160,512]{1,0:T(8,128)(2,1)S(1)}, u32[]{:S(2)}) copy-start(bf16[160,512]{1,0:T(8,128)(2,1)S(1)} %get-tuple-element.62.dq) | copy-start | bytes 491524
  130.4 11.5 %copy-start.21 = (bf16[160,512]{1,0:T(8,128)(2,1)}, bf16[160,512]{1,0:T(8,128)(2,1)S(1)}, u32[]{:S(2)}) copy-start(bf16[160,512]{1,0:T(8,128)(2,1)S(1)} %get-tuple-element.63.dk) | copy-start | bytes 491524
  130.4 11.5 %copy-start.23 = (bf16[160,512]{1,0:T(8,128)(2,1)}, bf16[160,512]{1,0:T(8,128)(2,1)S(1)}, u32[]{:S(2)}) copy-start(bf16[160,512]{1,0:T(8,128)(2,1)S(1)} %get-tuple-element.64.dv) | copy-start | bytes 491524
  130.4 11.4 %collective-permute-start.11 = (bf16[4,320,128]{2,1,0:T(8,128)(2,1)S(1)}, bf16[4,320,128]{2,1,0:T(8,128)(2,1)S(1)}, u32[]{:S(2)}, u32[]{:S(2)}) collective-permute-start(bf16[4,320,128]{2,1,0:T(8,128)(2,1)S(1)} %get-tuple-element.66), channel_id=1, source_target_pairs={{0,4},{4,8},{8,12},{12,16},{16,20},{20,24},{24,28},{28,32},{32,36}... | collective-permute-start | bytes 983048 | tf_op jit(solution)/shard_map/ppermute | solution.py:333
  141.9 28.6 %collective-permute-start.12 = (bf16[4,320,128]{2,1,0:T(8,128)(2,1)S(1)}, bf16[4,320,128]{2,1,0:T(8,128)(2,1)S(1)}, u32[]{:S(2)}, u32[]{:S(2)}) collective-permute-start(bf16[4,320,128]{2,1,0:T(8,128)(2,1)S(1)} %add.11), channel_id=1, source_target_pairs={{0,128},{4,132},{8,136},{12,140},{16,144},{20,148},{24,152},{28,15... | collective-permute-start | bytes 983048 | tf_op jit(solution)/shard_map/ppermute | solution.py:329
  163.6 1.2 copy-start.12
  (10 other events, 9.2 us)
